TPU v7x, 128 devices: a whole 4x4x4 slice. The times are simulated.
128 devices in a mesh: row: 16 (over x_hi, z, core), col: 8 (over y, x_lo).
Axes of the slice: x: 4 (x_hi: 2, x_lo: 2; x = x_hi * 2 + x_lo), y: 4, z: 4, core: 2. Of those that a mesh axis runs over, the one named last changes fastest.
Arguments:
- pair_in: float32 [384, 384, 128], P('row', 'col'), may hold values from -6 to 6
- cotangent: float32 [384, 384, 128], P('row', 'col'), may hold values from -6 to 6
- outgoing_proj: bfloat16 [128, 512], replicated, may hold values from -0.5 to 0.5
- outgoing_gate: bfloat16 [128, 128], replicated, may hold values from -0.5 to 0.5
- outgoing_lift: bfloat16 [128, 128], replicated, may hold values from -0.5 to 0.5
- incoming_proj: bfloat16 [128, 512], replicated, may hold values from -0.5 to 0.5
- incoming_gate: bfloat16 [128, 128], replicated, may hold values from -0.5 to 0.5
- incoming_lift: bfloat16 [128, 128], replicated, may hold values from -0.5 to 0.5
Outputs:
- pair_result: float32 [384, 384, 128], P('row', 'col')
- pair_grad: float32 [384, 384, 128], P('row', 'col')
- dproj_outgoing: float32 [128, 512], replicated
- dgate_outgoing: float32 [128, 128], replicated
- dlift_outgoing: float32 [128, 128], replicated
- dproj_incoming: float32 [128, 512], replicated
- dgate_incoming: float32 [128, 128], replicated
- dlift_incoming: float32 [128, 128], replicated
All inputs are finite; a program needn't handle non-finite values.
Results may differ from a plain program's by a relative error of at most 0.035.
Values may be sent and summed in bfloat16 or wider, within the bound.
A program may use at most 128 MiB of HBM per device.

v0:
```python
import jax
import jax.numpy as jnp
from jax import lax
from jax.sharding import PartitionSpec as P

EPSILON = 1e-05


def layer_norm(pair_field):
    mean_val = jnp.mean(pair_field, axis=-1, keepdims=True)
    centred = pair_field - mean_val
    spread = jnp.sqrt(jnp.mean(centred * centred, axis=-1, keepdims=True) + EPSILON)
    return (centred / spread, spread)


def norm_back(grad_in, normed, spread):
    mean_grad = jnp.mean(grad_in, axis=-1, keepdims=True)
    mean_mixed = jnp.mean(grad_in * normed, axis=-1, keepdims=True)
    return (grad_in - mean_grad - normed * mean_mixed) / spread


def flat_dot(first, matrix):
    lead_shape = first.shape[:-1]
    result = jnp.dot(first.reshape(-1, first.shape[-1]), matrix, preferred_element_type=jnp.float32)
    return result.reshape(lead_shape + (matrix.shape[-1],))


def cell_sum(first, second):
    return jnp.dot(
        first.reshape(-1, first.shape[-1]).T,
        second.reshape(-1, second.shape[-1]),
        preferred_element_type=jnp.float32,
    )


def project_tile(pair_field, w_proj, w_gate):
    normed, spread = layer_norm(pair_field)
    normed_b = normed.astype(jnp.bfloat16)
    pre_act = flat_dot(normed_b, w_proj)
    hidden_size = pre_act.shape[-1] // 4
    left_proj = (
        jax.nn.sigmoid(pre_act[..., :hidden_size]) * pre_act[..., hidden_size : 2 * hidden_size]
    ).astype(jnp.bfloat16)
    right_proj = (
        jax.nn.sigmoid(pre_act[..., 2 * hidden_size : 3 * hidden_size])
        * pre_act[..., 3 * hidden_size :]
    ).astype(jnp.bfloat16)
    gate_val = jax.nn.sigmoid(flat_dot(normed_b, w_gate))
    return (normed, spread, normed_b, pre_act, left_proj, right_proj, gate_val)


def finish_tile(tri_sum, gate_val, w_lift):
    unit, unit_spread = layer_norm(tri_sum)
    unit_b = unit.astype(jnp.bfloat16)
    lifted = flat_dot(unit_b, w_lift)
    return (gate_val * lifted, unit, unit_spread, unit_b, lifted)


def head_back(grad_out, gate_val, lifted, unit, unit_spread, unit_b, w_lift):
    grad_lift = (grad_out * gate_val).astype(jnp.bfloat16)
    grad_gate = (grad_out * lifted * gate_val * (1.0 - gate_val)).astype(jnp.bfloat16)
    grad_unit = flat_dot(grad_lift, w_lift.T)
    dlift = cell_sum(unit_b, grad_lift)
    grad_tri = norm_back(grad_unit, unit, unit_spread).astype(jnp.bfloat16)
    return (grad_tri, grad_gate, dlift)


def tail_back(
    grad_out, grad_gate, grad_left, grad_right, normed, spread, normed_b, pre_act, w_proj, w_gate
):
    hidden_size = pre_act.shape[-1] // 4
    sig_left = jax.nn.sigmoid(pre_act[..., :hidden_size])
    sig_right = jax.nn.sigmoid(pre_act[..., 2 * hidden_size : 3 * hidden_size])
    grad_pre = jnp.concatenate(
        [
            grad_left * pre_act[..., hidden_size : 2 * hidden_size] * sig_left * (1.0 - sig_left),
            grad_left * sig_left,
            grad_right * pre_act[..., 3 * hidden_size :] * sig_right * (1.0 - sig_right),
            grad_right * sig_right,
        ],
        axis=-1,
    ).astype(jnp.bfloat16)
    grad_normed = flat_dot(grad_pre, w_proj.T) + flat_dot(grad_gate, w_gate.T)
    grad_field = grad_out + norm_back(grad_normed, normed, spread)
    return (grad_field, cell_sum(normed_b, grad_pre), cell_sum(normed_b, grad_gate))


def local(
    pair_in,
    cotangent,
    outgoing_proj,
    outgoing_gate,
    outgoing_lift,
    incoming_proj,
    incoming_gate,
    incoming_lift,
):
    normed_a, spread_a, normed_ab, pre_a, left_a, right_a, gate_a = project_tile(
        pair_in, outgoing_proj, outgoing_gate
    )
    right_cols = lax.all_gather(right_a, "row", axis=0, tiled=True)
    block = right_cols
    tri_flip = lax.psum_scatter(
        jnp.einsum("jkh,ikh->jih", block, left_a, preferred_element_type=jnp.float32).astype(
            jnp.bfloat16
        ),
        "col",
        scatter_dimension=0,
        tiled=True,
    ).astype(jnp.float32)
    tri_a = jnp.transpose(tri_flip, (1, 0, 2))
    update_a, unit_a, unit_spread_a, unit_ab, lifted_a = finish_tile(tri_a, gate_a, outgoing_lift)
    middle = pair_in + update_a
    normed_c, spread_c, normed_cb, pre_c, left_c, right_c, gate_c = project_tile(
        middle, incoming_proj, incoming_gate
    )
    left_rows = lax.all_gather(left_c, "col", axis=1, tiled=True)
    block = left_rows
    tri_c = lax.psum_scatter(
        jnp.einsum("kih,kjh->ijh", block, right_c, preferred_element_type=jnp.float32).astype(
            jnp.bfloat16
        ),
        "row",
        scatter_dimension=0,
        tiled=True,
    ).astype(jnp.float32)
    update_c, unit_c, unit_spread_c, unit_cb, lifted_c = finish_tile(tri_c, gate_c, incoming_lift)
    pair_result = middle + update_c
    grad_tri_c, grad_gate_c, dlift_inc = head_back(
        cotangent, gate_c, lifted_c, unit_c, unit_spread_c, unit_cb, incoming_lift
    )
    tri_cols = lax.all_gather(grad_tri_c, "row", axis=0, tiled=True)
    grad_right_c = jnp.einsum(
        "kih,ijh->kjh", left_rows, tri_cols, preferred_element_type=jnp.float32
    )
    block = tri_cols
    grad_left_flip = lax.psum_scatter(
        jnp.einsum("ijh,kjh->ikh", block, right_c, preferred_element_type=jnp.float32).astype(
            jnp.bfloat16
        ),
        "col",
        scatter_dimension=0,
        tiled=True,
    ).astype(jnp.float32)
    grad_left_c = jnp.transpose(grad_left_flip, (1, 0, 2))
    grad_middle, dproj_inc, dgate_inc = tail_back(
        cotangent,
        grad_gate_c,
        grad_left_c,
        grad_right_c,
        normed_c,
        spread_c,
        normed_cb,
        pre_c,
        incoming_proj,
        incoming_gate,
    )
    grad_tri_a, grad_gate_a, dlift_out = head_back(
        grad_middle, gate_a, lifted_a, unit_a, unit_spread_a, unit_ab, outgoing_lift
    )
    tri_rows = lax.all_gather(grad_tri_a, "col", axis=1, tiled=True)
    grad_left_a = jnp.einsum(
        "ijh,jkh->ikh", tri_rows, right_cols, preferred_element_type=jnp.float32
    )
    block = tri_rows
    grad_right_a = lax.psum_scatter(
        jnp.einsum("ijh,ikh->jkh", block, left_a, preferred_element_type=jnp.float32).astype(
            jnp.bfloat16
        ),
        "row",
        scatter_dimension=0,
        tiled=True,
    ).astype(jnp.float32)
    pair_grad, dproj_out, dgate_out = tail_back(
        grad_middle,
        grad_gate_a,
        grad_left_a,
        grad_right_a,
        normed_a,
        spread_a,
        normed_ab,
        pre_a,
        outgoing_proj,
        outgoing_gate,
    )
    summed = lax.psum(
        (dproj_out, dgate_out, dlift_out, dproj_inc, dgate_inc, dlift_inc), ("row", "col")
    )
    return (
        pair_result,
        pair_grad,
        summed[0],
        summed[1],
        summed[2],
        summed[3],
        summed[4],
        summed[5],
    )


def solution(mesh):
    in_specs = (P("row", "col", None), P("row", "col", None), P(), P(), P(), P(), P(), P())
    out_specs = (P("row", "col", None), P("row", "col", None), P(), P(), P(), P(), P(), P())
    return jax.shard_map(local, mesh=mesh, in_specs=in_specs, out_specs=out_specs, check_vma=False)
```

profile of v0, /device:TPU:1, one launch (start us, length us, event | category | flops | bytes accessed | tf_op | source)
XLA Modules:
  0.0 819.0 jit_solution(10265137046796191238)
XLA Ops:
  16.2 60.1 %all-gather.5.cloned.1.call-done = bf16[384,48,128]{2,1,0:T(8,128)(2,1)} async-done(((bf16[24,48,128]{2,1,0:T(8,128)(2,1)}), bf16[384,48,128]{2,1,0:T(8,128)(2,1)}) %all-gather.5.cloned.1.call-update) | async-done | bytes 4718608 | tf_op jit(solution)/shard_map/all_gather | solution.py:101
  76.2 17.8 %copy.82 = bf16[384,48,128]{1,0,2:T(8,128)(2,1)} copy(bf16[384,48,128]{2,1,0:T(8,128)(2,1)} %all-gather.5.cloned.1.call-done) | data formatting | bytes 9437184 | tf_op jit(solution)/shard_map/all_gather | solution.py:101
  94.1 10.4 %convert_bitcast_fusion.3 = bf16[384,24,128]{0,1,2:T(8,128)(2,1)} fusion(bf16[24,48,128]{1,0,2:T(8,128)(2,1)S(1)} %copy.81, bf16[384,48,128]{1,0,2:T(8,128)(2,1)} %copy.82), kind=kOutput, calls=%fused_computation.3 | convolution fusion | flops 114425856 | bytes 7372800 | tf_op jit(solution)/shard_map/jkh,ikh->jih/dot_general | solution.py:104
  104.5 4.7 copy.83
  109.2 54.5 %reduce-scatter.5.cloned.1.call-done = bf16[48,24,128]{2,1,0:T(8,128)(2,1)} async-done(((bf16[384,24,128]{2,1,0:T(8,128)(2,1)}), bf16[48,24,128]{2,1,0:T(8,128)(2,1)}) %reduce-scatter.5.cloned.1.call-update) | async-done | bytes 294928 | tf_op jit(solution)/shard_map/reduce_scatter | solution.py:103
  175.3 54.9 %all-gather.7.cloned.1.call-done = bf16[24,384,128]{2,1,0:T(8,128)(2,1)} async-done(((bf16[24,48,128]{2,1,0:T(8,128)(2,1)}), bf16[24,384,128]{2,1,0:T(8,128)(2,1)}) %all-gather.7.cloned.1.call-update) | async-done | bytes 2359312 | tf_op jit(solution)/shard_map/all_gather | solution.py:117
  230.2 4.5 copy.86
  234.7 5.5 convert_bitcast_fusion.1
  240.3 7.6 copy.87
  247.9 81.3 %reduce-scatter.7.cloned.1.call-done = bf16[24,48,128]{2,1,0:T(8,128)(2,1)} async-done(((bf16[384,48,128]{2,1,0:T(8,128)(2,1)}), bf16[24,48,128]{2,1,0:T(8,128)(2,1)}) %reduce-scatter.7.cloned.1.call-update) | async-done | bytes 294928 | tf_op jit(solution)/shard_map/reduce_scatter | solution.py:119
  337.3 58.2 %all-gather.9.cloned.1.call-done = bf16[384,48,128]{2,1,0:T(8,128)(2,1)} async-done(((bf16[24,48,128]{2,1,0:T(8,128)(2,1)}), bf16[384,48,128]{2,1,0:T(8,128)(2,1)}) %all-gather.9.cloned.1.call-update) | async-done | bytes 4718608 | tf_op jit(solution)/shard_map/all_gather | solution.py:132
  395.4 17.8 %copy.95 = bf16[384,48,128]{1,0,2:T(8,128)(2,1)} copy(bf16[384,48,128]{2,1,0:T(8,128)(2,1)} %all-gather.9.cloned.1.call-done) | data formatting | bytes 9437184 | tf_op jit(solution)/shard_map/all_gather | solution.py:132
  413.3 10.8 %fusion.79 = bf16[128,24,384]{2,1,0:T(8,128)(2,1)} fusion(bf16[24,48,128]{1,0,2:T(8,128)(2,1)} %copy.85, bf16[384,48,128]{1,0,2:T(8,128)(2,1)} %copy.95), kind=kOutput, calls=%fused_computation.145 | convolution fusion | flops 113246208 | bytes 7372800 | tf_op jit(solution)/shard_map/ijh,kjh->ikh/dot_general | solution.py:138
  424.1 4.5 copy.96
  428.9 8.7 %fusion.80 = f32[128,48,24]{1,2,0:T(8,128)} fusion(bf16[384,48,128]{1,0,2:T(8,128)(2,1)} %copy.95, bf16[24,384,128]{1,0,2:T(8,128)(2,1)} %copy.86), kind=kOutput, calls=%fused_computation.146 | convolution fusion | flops 113246208 | bytes 7667712 | tf_op jit(solution)/shard_map/kih,ijh->kjh/dot_general | solution.py:133
  437.6 2.7 copy.99
  440.3 42.9 %reduce-scatter.9.cloned.1.call-done = bf16[48,24,128]{2,0,1:T(8,128)(2,1)} async-done(((bf16[384,24,128]{2,0,1:T(8,128)(2,1)}), bf16[48,24,128]{2,0,1:T(8,128)(2,1)}) %reduce-scatter.9.cloned.1.call-update) | async-done | bytes 294928 | tf_op jit(solution)/shard_map/reduce_scatter | solution.py:137
  483.2 2.4 fusion.35
  492.5 56.3 %all-gather.11.cloned.1.call-done = bf16[24,384,128]{2,0,1:T(8,128)(2,1)} async-done(((bf16[24,48,128]{2,0,1:T(8,128)(2,1)}), bf16[24,384,128]{2,0,1:T(8,128)(2,1)}) %all-gather.11.cloned.1.call-update) | async-done | bytes 2359312 | tf_op jit(solution)/shard_map/all_gather | solution.py:161
  548.8 4.8 copy.102
  553.6 5.5 fusion.82
  559.1 7.6 copy.106
  567.0 2.0 convolution_bitcast_fusion.3
  569.1 2.3 convolution_bitcast_fusion.2
  574.7 9.4 %fusion.81 = f32[128,48,24]{1,2,0:T(8,128)} fusion(bf16[384,48,128]{1,0,2:T(8,128)(2,1)} %copy.82, bf16[24,384,128]{1,0,2:T(8,128)(2,1)} %copy.102), kind=kOutput, calls=%fused_computation.147 | convolution fusion | flops 113246208 | bytes 7667712 | tf_op jit(solution)/shard_map/ijh,jkh->ikh/dot_general | solution.py:162
  584.1 2.8 copy.103
  586.9 61.2 %reduce-scatter.11.cloned.1.call-done = bf16[24,48,128]{2,1,0:T(8,128)(2,1)} async-done(((bf16[384,48,128]{2,1,0:T(8,128)(2,1)}), bf16[24,48,128]{2,1,0:T(8,128)(2,1)}) %reduce-scatter.11.cloned.1.call-update) | async-done | bytes 294928 | tf_op jit(solution)/shard_map/reduce_scatter | solution.py:166
  648.1 1.6 fusion.27
  651.9 1.7 fusion.40
  656.2 147.1 %all-reduce.3.cloned.1.call-done = (f32[128,512]{1,0:T(8,128)}, f32[128,128]{1,0:T(8,128)}, f32[128,128]{1,0:T(8,128)}, f32[128,512]{1,0:T(8,128)}, f32[128,128]{1,0:T(8,128)}, /*index=5*/f32[128,128]{1,0:T(8,128)}) async-done(((f32[128,512]{1,0:T(8,128)}, f32[128,128]{1,0:T(8,128)}, f32[128,128]{1,0:T(8,128)}, f32[128,512]{1,0:T(8,128)}, f32[128,128]{1,0:T(8,128)}, /*index=5*/f32[128,128]{1,0:T(8,128)}), ...) | async-done | bytes 786448 | tf_op jit(solution)/shard_map/psum | solution.py:186
  803.3 1.7 copy.129
  807.9 1.7 copy.132
  (167 shorter events, 49.4 us)
Async XLA Ops:
  7.2 163.8 %copy-start = (bf16[128,512]{1,0:T(8,128)(2,1)S(1)}, bf16[128,512]{1,0:T(8,128)(2,1)}, u32[]{:S(2)}) copy-start(bf16[128,512]{1,0:T(8,128)(2,1)} %param.13) | copy-start | bytes 393220
  7.2 69.1 %all-gather.5.cloned.1.call-start = ((), (), s32[]{:S(2)}) async-start(), calls=%async_computation.4 | async-start | bytes 5013504 | tf_op jit(solution)/shard_map/all_gather | solution.py:101
  14.7 149.0 %reduce-scatter.5.cloned.1.call-start = ((), (), s32[]{:S(2)}) async-start(), calls=%async_computation.5 | async-start | bytes 2654208 | tf_op jit(solution)/shard_map/reduce_scatter | solution.py:103
  16.2 77.9 %copy-start.3 = (bf16[24,48,128]{1,0,2:T(8,128)(2,1)}, bf16[24,48,128]{1,0,2:T(8,128)(2,1)S(1)}, u32[]{:S(2)}) copy-start(bf16[24,48,128]{1,0,2:T(8,128)(2,1)S(1)} %copy.81) | copy-start | bytes 884740
  109.1 57.2 %copy-start.42 = (bf16[128,128]{1,0:T(8,128)(2,1)S(1)}, bf16[128,128]{1,0:T(8,128)(2,1)}, u32[]{:S(2)}) copy-start(bf16[128,128]{1,0:T(8,128)(2,1)} %param.12) | copy-start | bytes 98308
  109.1 58.7 %copy-start.2 = (f32[24,48,128]{2,1,0:T(8,128)S(1)}, f32[24,48,128]{2,1,0:T(8,128)}, u32[]{:S(2)}) copy-start(f32[24,48,128]{2,1,0:T(8,128)} %param.8) | copy-start | bytes 1769476
  109.1 58.7 %copy-start.13 = (bf16[24,48,128]{2,1,0:T(8,128)(2,1)S(1)}, bf16[24,48,128]{2,1,0:T(8,128)(2,1)}, u32[]{:S(2)}) copy-start(bf16[24,48,128]{2,1,0:T(8,128)(2,1)} %copy-done.12) | copy-start | bytes 884740
  109.1 58.7 %copy-start.44 = (bf16[128,128]{1,0:T(8,128)(2,1)S(1)}, bf16[128,128]{1,0:T(8,128)(2,1)}, u32[]{:S(2)}) copy-start(bf16[128,128]{1,0:T(8,128)(2,1)} %param.11) | copy-start | bytes 98308
  109.2 121.1 %all-gather.7.cloned.1.call-start = ((), (), s32[]{:S(2)}) async-start(), calls=%async_computation.6 | async-start | bytes 2654208 | tf_op jit(solution)/shard_map/all_gather | solution.py:117
  173.8 155.4 %reduce-scatter.7.cloned.1.call-start = ((), (), s32[]{:S(2)}) async-start(), calls=%async_computation.7 | async-start | bytes 5013504 | tf_op jit(solution)/shard_map/reduce_scatter | solution.py:119
  247.8 84.1 %copy-start.40 = (bf16[128,128]{1,0:T(8,128)(2,1)S(1)}, bf16[128,128]{1,0:T(8,128)(2,1)}, u32[]{:S(2)}) copy-start(bf16[128,128]{1,0:T(8,128)(2,1)} %param.15) | copy-start | bytes 98308
  247.8 85.6 %copy-start.17 = (bf16[24,48,128]{2,1,0:T(8,128)(2,1)S(1)}, bf16[24,48,128]{2,1,0:T(8,128)(2,1)}, u32[]{:S(2)}) copy-start(bf16[24,48,128]{2,1,0:T(8,128)(2,1)} %copy-done.16) | copy-start | bytes 884740
  247.9 85.6 %copy-start.41 = (bf16[128,128]{1,0:T(8,128)(2,1)S(1)}, bf16[128,128]{1,0:T(8,128)(2,1)}, u32[]{:S(2)}) copy-start(bf16[128,128]{1,0:T(8,128)(2,1)} %param.14) | copy-start | bytes 98308
  247.9 147.6 %all-gather.9.cloned.1.call-start = ((), (), s32[]{:S(2)}) async-start(), calls=%async_computation.8 | async-start | bytes 5013504 | tf_op jit(solution)/shard_map/all_gather | solution.py:132
  329.2 4.2 copy-start.5
  329.2 4.2 copy-start.19
  337.2 146.0 %reduce-scatter.9.cloned.1.call-start = ((), (), s32[]{:S(2)}) async-start(), calls=%async_computation.9 | async-start | bytes 2654208 | tf_op jit(solution)/shard_map/reduce_scatter | solution.py:137
  428.6 120.2 %all-gather.11.cloned.1.call-start = ((), (), s32[]{:S(2)}) async-start(), calls=%async_computation.10 | async-start | bytes 2654208 | tf_op jit(solution)/shard_map/all_gather | solution.py:161
  485.7 2.4 copy-start.27
  485.7 2.4 copy-start.29
  492.4 155.7 %reduce-scatter.11.cloned.1.call-start = ((), (), s32[]{:S(2)}) async-start(), calls=%async_computation.11 | async-start | bytes 5013504 | tf_op jit(solution)/shard_map/reduce_scatter | solution.py:166
  566.7 236.6 %all-reduce.3.cloned.1.call-start = ((), (), s32[]{:S(2)}) async-start(), calls=%async_computation.12 | async-start | bytes 1572864 | tf_op jit(solution)/shard_map/psum | solution.py:186
  567.0 4.4 copy-start.14
  567.0 4.4 copy-start.37
  567.0 5.3 copy-start.36
  571.4 2.2 copy-start.18
  571.4 2.2 copy-start.24
  571.4 2.2 copy-start.26
  571.4 2.2 copy-start.28
  571.4 2.2 copy-start.30
  586.9 63.9 %copy-start.15 = (bf16[24,48,128]{2,1,0:T(8,128)(2,1)S(1)}, bf16[24,48,128]{2,1,0:T(8,128)(2,1)}, u32[]{:S(2)}) copy-start(bf16[24,48,128]{2,1,0:T(8,128)(2,1)} %copy-done.12) | copy-start | bytes 884740
  649.8 2.1 copy-start.39
  (25 other events, 32.0 us)
Sparse Core Ops, SparseCore 0:
  14.9 61.3 all-gather.4
  109.3 54.4 reduce-scatter.4
  174.0 56.2 all-gather.6
  248.0 81.2 reduce-scatter.6
  337.3 58.0 all-gather.8
  428.7 54.4 reduce-scatter.8
  492.5 56.2 all-gather.10
  566.8 81.2 reduce-scatter.10
  654.7 148.5 all-reduce.2
where the time goes:
time: 821 us; the launch traced here: 819 us
  waiting for transfers between devices  617 us (75%)
  local copies, waits for them, and re-layouts  92.8 us (11%)
  matrix products  72 us (9%)
  other arithmetic  21.9 us (3%)
  between operations  14.6 us (2%)
    psum x1, waiting for transfers between devices, local(): lax.psum((dproj_out, dgate_out, dlift_out, dproj_inc, dgate_inc, dlift_in...  147 us
    reduce_scatter x1, waiting for transfers between devices, local(): lax.psum_scatter(jnp.einsum('kih,kjh->ijh', block, right_c, preferred_ele...  81.3 us
    reduce_scatter x1, waiting for transfers between devices, local(): lax.psum_scatter(jnp.einsum('ijh,ikh->jkh', block, left_a, preferred_elem...  61.2 us
    all_gather x1, waiting for transfers between devices, local(): right_cols = lax.all_gather(right_a, 'row', axis=0, tiled=True)  60.1 us
    all_gather x1, waiting for transfers between devices, local(): tri_cols = lax.all_gather(grad_tri_c, 'row', axis=0, tiled=True)  58.2 us
    all_gather x1, waiting for transfers between devices, local(): tri_rows = lax.all_gather(grad_tri_a, 'col', axis=1, tiled=True)  56.3 us
    all_gather x1, waiting for transfers between devices, local(): left_rows = lax.all_gather(left_c, 'col', axis=1, tiled=True)  54.9 us
    reduce_scatter x1, waiting for transfers between devices, local(): lax.psum_scatter(jnp.einsum('jkh,ikh->jih', block, left_a, preferred_elem...  54.5 us
  transfers between devices with their start and end apart: 9, of which 9 were waited for; matrix products, arithmetic and copies ran while one was open for 4% of the time, Pallas kernels for 0%

commit v1 on v0

v1 whole, which is shorter than its diff:
```python
import types

import jax
import jax.numpy as jnp
from jax import lax
from jax.experimental import pallas as pl
from jax.experimental.pallas import tpu as pltpu
from jax.sharding import PartitionSpec as P

F32 = jnp.float32
BF16 = jnp.bfloat16
EPSILON = 1e-05
MESH = pl.DeviceIdType.MESH

ROWS, COLS, DEVICES = 16, 8, 128
BI, BK, C = 24, 48, 128
TILES = 12
SLOT = 64
WIDE = COLS * SLOT
CELLS = TILES * 128
DBL, SGL, GRD = 24, 16, 8

MODULE_FIELDS = ("n", "s1", "p2", "s3", "p4", "gate", "u", "lifted")
FLAT_FIELDS = ("nb", "ub", "gl", "gg")


def dot(a, b, ca=1, cb=0):
    return lax.dot_general(a, b, (((ca,), (cb,)), ((), ())), preferred_element_type=F32)


def norm(p):
    d = p - jnp.mean(p, axis=0, keepdims=True)
    r = lax.rsqrt(jnp.mean(d * d, axis=0, keepdims=True) + EPSILON)
    return d * r, r


def norm_back(q, n, r):
    return (q - jnp.mean(q, axis=0, keepdims=True) - n * jnp.mean(q * n, axis=0, keepdims=True)) * r


def lanes(t):
    return pl.ds(pl.multiple_of(t * 128, 128), 128)


def kernel(*refs):
    (pair, cot, wp_o, wg_o, wl_o, wp_i, wg_i, wl_i, res, grad, dpo, dgo, dlo, dpi, dgi, dli) = refs[:16]
    it = iter(refs[16:])

    def module(wp, wg, wl):
        m = types.SimpleNamespace(wp=wp, wg=wg, wl=wl)
        for name in MODULE_FIELDS + FLAT_FIELDS + ("gp", "r", "ur", "wpt", "wgt", "wlt", "ml", "mr", "ws", "wr", "wa"):
            setattr(m, name, next(it))
        return m

    out, inc = module(wp_o, wg_o, wl_o), module(wp_i, wg_i, wl_i)
    xt, ct, mt, gt, stage, gmat, snd_d, rec_d, snd_s, rec_s, ssem, rsem = it

    row, col = lax.axis_index("row"), lax.axis_index("col")
    me = row * COLS + col
    cols = [lax.rem(col + b, COLS) for b in range(COLS)]

    def peers(visit):
        def step(a, carry):
            rr = lax.rem(row + a, ROWS)
            for b in range(COLS):
                if b:
                    visit(rr, cols[b])
                else:
                    @pl.when(a > 0)
                    def _():
                        visit(rr, cols[0])
            return carry

        lax.fori_loop(0, ROWS, step, 0)

    barrier = pltpu.get_barrier_semaphore()
    peers(lambda rr, cc: pl.semaphore_signal(barrier, inc=1, device_id=(rr, cc), device_id_type=MESH))

    def start(src, dst, k, rr, cc):
        pltpu.make_async_remote_copy(
            src, dst, ssem.at[k], rsem.at[k], device_id=(rr, cc), device_id_type=MESH
        ).start()

    def drain(ref, sem, k):
        span = ref.at[pl.ds(0, DEVICES - 1)]
        pltpu.make_async_copy(span, span, sem.at[k]).wait()

    def arrive(ref, k):
        drain(ref, rsem, k)

    def send_staged(snd, dst, k, size):
        def piece(p):
            return stage[pl.ds(pl.multiple_of(p * size, 8), size), :].astype(BF16)

        def visit(rr, cc):
            p = rr * COLS + cc
            snd[p] = piece(p)
            start(snd.at[p], dst.at[me], k, rr, cc)

        peers(visit)
        dst[me] = piece(me)

    def send_ready(snd, dst, k):
        peers(lambda rr, cc: start(snd.at[rr * COLS + cc], dst.at[me], k, rr, cc))
        dst[me] = snd[me]

    def unpack(rec, size):
        def step(a, carry):
            for b in range(COLS):
                p = a * COLS + b
                stage[pl.ds(pl.multiple_of(p * size, 8), size), :] = rec[p].astype(F32)
            return carry

        lax.fori_loop(0, ROWS, step, 0)

    def tiles(body):
        lax.fori_loop(0, TILES, lambda t, carry: (body(t), carry)[1], 0)

    low = lax.broadcasted_iota(jnp.int32, (BI, 128), 1) < SLOT
    top = lax.broadcasted_iota(jnp.int32, (BI, 128), 0) < TILES
    gap8 = jnp.zeros((8, 128), F32)
    gap16 = jnp.zeros((16, 128), F32)

    def swap_lanes(a):
        return pltpu.roll(a, SLOT, 1)

    def swap_rows(a):
        return pltpu.roll(a, TILES, 0)

    def halves(a, b):
        return jnp.where(low, a, swap_lanes(b)), jnp.where(low, swap_lanes(a), b)

    def assemble_double(rec, left, right):
        def step(r2, carry):
            at = pl.ds(pl.multiple_of(r2 * SLOT, SLOT), SLOT)
            for m in range(COLS // 2):
                ls, rs = [], []
                for s in range(2):
                    p = (2 * r2 + s) * COLS + 2 * m
                    o0, o1 = halves(rec[p].astype(F32), rec[p + 1].astype(F32))
                    ls.append(jnp.where(top, o0, swap_rows(o1)))
                    rs.append(jnp.where(top, swap_rows(o0), o1))
                left[at, m * 128 : (m + 1) * 128] = jnp.concatenate(ls + [gap16], axis=0).astype(BF16)
                right[at, m * 128 : (m + 1) * 128] = jnp.concatenate(rs + [gap16], axis=0).astype(BF16)
            return carry

        lax.fori_loop(0, ROWS // 2, step, 0)

    def assemble_single(rec, whole):
        def step(r2, carry):
            at = pl.ds(pl.multiple_of(r2 * SLOT, SLOT), SLOT)
            for m in range(COLS // 2):
                ls = []
                for s in range(2):
                    p = (2 * r2 + s) * COLS + 2 * m
                    a, b = (jnp.concatenate([rec[q].astype(F32), gap8], axis=0) for q in (p, p + 1))
                    o0, o1 = halves(a, b)
                    ls.append(jnp.where(top, o0, swap_rows(o1)))
                whole[at, m * 128 : (m + 1) * 128] = jnp.concatenate(ls + [gap16], axis=0).astype(BF16)
            return carry

        lax.fori_loop(0, ROWS // 2, step, 0)

    def cut(block, upper):
        turned = swap_rows(block)
        first, second = (turned, block) if upper else (block, turned)
        return jnp.where(low, first, swap_lanes(second)), jnp.where(low, swap_lanes(first), second)

    def split_rows(rows_of, snd):
        def step(q, carry):
            blocks = rows_of(pl.ds(pl.multiple_of(q * 128, 128), 128))
            for s4 in range(4):
                lo = SLOT * (s4 // 2) + BI * (s4 % 2)
                for m in range(COLS // 2):
                    p = (4 * q + s4) * COLS + 2 * m
                    ms = [cut(b[lo : lo + BI, m * 128 : (m + 1) * 128], j) for j, b in enumerate(blocks)]
                    if len(ms) == 1:
                        snd[p] = ms[0][0][:SGL].astype(BF16)
                        snd[p + 1] = ms[0][1][:SGL].astype(BF16)
                    else:
                        snd[p] = jnp.where(top, ms[0][0], ms[1][0]).astype(BF16)
                        snd[p + 1] = jnp.where(top, ms[0][1], ms[1][1]).astype(BF16)
            return carry

        lax.fori_loop(0, WIDE // 128, step, 0)

    def into_tiles(src, dst):
        def body(t):
            rows = jnp.concatenate([src[t], gap16, src[TILES + t], gap16], axis=0)
            dst[t] = rows.T

        tiles(body)

    def out_tile(t, value, dst):
        back = value.T
        dst[t] = back[:BK]
        dst[TILES + t] = back[SLOT : SLOT + BK]

    def strided(t, size):
        return stage[pl.ds(t, 128, stride=size), :]

    def project(t, x, m):
        n, r = norm(x)
        nb = n.astype(BF16)
        m.n[t] = n
        m.r[t] = jnp.broadcast_to(r, (8, 128))
        m.nb[:, lanes(t)] = nb
        wpt = m.wpt
        s1 = jax.nn.sigmoid(dot(wpt[0:128], nb))
        p2 = dot(wpt[128:256], nb)
        m.s1[t] = s1
        m.p2[t] = p2
        stage[pl.ds(t, 128, stride=DBL), :] = s1 * p2
        s3 = jax.nn.sigmoid(dot(wpt[256:384], nb))
        p4 = dot(wpt[384:512], nb)
        m.s3[t] = s3
        m.p4[t] = p4
        stage[pl.ds(TILES + t, 128, stride=DBL), :] = s3 * p4
        m.gate[t] = jax.nn.sigmoid(dot(m.wgt[...], nb))

    def finish(t, tri, base, m):
        u, r = norm(tri)
        ub = u.astype(BF16)
        m.u[t] = u
        m.ur[t] = jnp.broadcast_to(r, (8, 128))
        m.ub[:, lanes(t)] = ub
        lifted = dot(m.wlt[...], ub)
        m.lifted[t] = lifted
        return base + m.gate[t] * lifted

    def head_back(t, g, m):
        gate = m.gate[t]
        through = g * gate
        gl = through.astype(BF16)
        m.gl[:, lanes(t)] = gl
        m.gg[:, lanes(t)] = (through * m.lifted[t] * (1.0 - gate)).astype(BF16)
        gunit = dot(m.wl[...], gl)
        stage[pl.ds(t, 128, stride=SGL), :] = norm_back(gunit, m.u[t], m.ur[t][0:1])

    def pre_back(t, m):
        gl, gr = strided(t, DBL), strided(TILES + t, DBL)
        s1, s3 = m.s1[t], m.s3[t]
        a, b = gl * s1, gr * s3
        m.gp[0:128, lanes(t)] = (a * m.p2[t] * (1.0 - s1)).astype(BF16)
        m.gp[128:256, lanes(t)] = a.astype(BF16)
        m.gp[256:384, lanes(t)] = (b * m.p4[t] * (1.0 - s3)).astype(BF16)
        m.gp[384:512, lanes(t)] = b.astype(BF16)

    def tail_back(t, g, m):
        gn = dot(m.wp[...], m.gp[:, lanes(t)]) + dot(m.wg[...], m.gg[:, lanes(t)])
        return g + norm_back(gn, m.n[t], m.r[t][0:1])

    def weight_rows(m, j, value):
        m.ws[pl.ds(j, 128, stride=GRD), :] = value

    def small_grads(m):
        weight_rows(m, 4, dot(m.nb[...], m.gg[...], 1, 1))
        weight_rows(m, 5, dot(m.ub[...], m.gl[...], 1, 1))

    def proj_grads(m):
        for j in range(4):
            weight_rows(m, j, dot(m.nb[...], m.gp[j * 128 : (j + 1) * 128, :], 1, 1))

    def part(ref, p):
        return ref.at[pl.ds(pl.multiple_of(p * GRD, GRD), GRD)]

    def scatter_grads(m, k):
        peers(lambda rr, cc: start(part(m.ws, rr * COLS + cc), m.wr.at[me], k, rr, cc))
        m.wr[me] = m.ws[pl.ds(pl.multiple_of(me * GRD, GRD), GRD), :]

    def gather_grads(m, k):
        arrive(m.wr, k)
        total = lax.fori_loop(
            0, ROWS, lambda a, acc: acc + jnp.sum(m.wr[pl.ds(a * COLS, COLS)], axis=0), jnp.zeros((GRD, 128), F32)
        )
        m.wa[pl.ds(pl.multiple_of(me * GRD, GRD), GRD), :] = total
        peers(lambda rr, cc: start(part(m.wa, me), part(m.wa, me), k + 1, rr, cc))

    def write_grads(m, k, dp, dg, dl):
        span = m.wa.at[pl.ds(0, (DEVICES - 1) * GRD)]
        pltpu.make_async_copy(span, span, rsem.at[k + 1]).wait()
        for j in range(4):
            dp[:, j * 128 : (j + 1) * 128] = m.wa[pl.ds(j, 128, stride=GRD), :]
        dg[...] = m.wa[pl.ds(4, 128, stride=GRD), :]
        dl[...] = m.wa[pl.ds(5, 128, stride=GRD), :]

    for m in (out, inc):
        m.wpt[...] = m.wp[...].T
        m.wgt[...] = m.wg[...].T
        m.wlt[...] = m.wl[...].T
        m.ws[...] = jnp.zeros(m.ws.shape, F32)
    into_tiles(pair, xt)
    tiles(lambda t: project(t, xt[t], out))
    pl.semaphore_wait(barrier, DEVICES - 1)
    send_staged(snd_d.at[0], rec_d.at[0], 0, DBL)
    into_tiles(cot, ct)
    arrive(rec_d.at[0], 0)
    assemble_double(rec_d.at[0], out.ml, out.mr)
    split_rows(lambda at: [dot(out.ml[at, :], out.mr[...], 1, 1)], snd_s.at[0])
    send_ready(snd_s.at[0], rec_s.at[0], 1)
    arrive(rec_s.at[0], 1)
    unpack(rec_s.at[0], SGL)

    def middle_tile(t):
        mid = finish(t, strided(t, SGL), xt[t], out)
        mt[t] = mid

    tiles(middle_tile)
    tiles(lambda t: project(t, mt[t], inc))
    send_staged(snd_d.at[1], rec_d.at[1], 2, DBL)
    arrive(rec_d.at[1], 2)
    assemble_double(rec_d.at[1], inc.ml, inc.mr)
    split_rows(lambda at: [dot(inc.ml[:, at], inc.mr[...], 0, 0)], snd_s.at[1])
    send_ready(snd_s.at[1], rec_s.at[1], 3)
    arrive(rec_s.at[1], 3)
    unpack(rec_s.at[1], SGL)

    def result_tile(t):
        mt[t] = finish(t, strided(t, SGL), mt[t], inc)
        head_back(t, ct[t], inc)

    tiles(result_tile)
    send_staged(snd_s.at[2], rec_s.at[2], 4, SGL)
    tiles(lambda t: out_tile(t, mt[t], res))
    arrive(rec_s.at[2], 4)
    assemble_single(rec_s.at[2], gmat)
    split_rows(
        lambda at: [dot(inc.mr[at, :], gmat[...], 1, 1), dot(inc.ml[at, :], gmat[...], 1, 0)], snd_d.at[2]
    )
    send_ready(snd_d.at[2], rec_d.at[2], 5)
    small_grads(inc)
    arrive(rec_d.at[2], 5)
    unpack(rec_d.at[2], DBL)

    tiles(lambda t: pre_back(t, inc))

    def grad_middle_tile(t):
        g = tail_back(t, ct[t], inc)
        gt[t] = g
        head_back(t, g, out)

    tiles(grad_middle_tile)
    send_staged(snd_s.at[3], rec_s.at[3], 6, SGL)
    proj_grads(inc)
    scatter_grads(inc, 8)
    arrive(rec_s.at[3], 6)
    assemble_single(rec_s.at[3], gmat)
    split_rows(
        lambda at: [dot(gmat[at, :], out.mr[...], 1, 0), dot(gmat[:, at], out.ml[...], 0, 0)], snd_d.at[3]
    )
    send_ready(snd_d.at[3], rec_d.at[3], 7)
    small_grads(out)
    gather_grads(inc, 8)
    arrive(rec_d.at[3], 7)
    unpack(rec_d.at[3], DBL)
    tiles(lambda t: pre_back(t, out))
    proj_grads(out)
    scatter_grads(out, 10)
    tiles(lambda t: out_tile(t, tail_back(t, gt[t], out), grad))
    write_grads(inc, 8, dpi, dgi, dli)
    gather_grads(out, 10)
    write_grads(out, 10, dpo, dgo, dlo)

    for j, k in enumerate((0, 2, 5, 7)):
        drain(snd_d.at[j], ssem, k)
    for j, k in enumerate((1, 3, 4, 6)):
        drain(snd_s.at[j], ssem, k)
    for m, k in ((inc, 8), (out, 10)):
        drain(m.wr, ssem, k)
        drain(m.wr, ssem, k + 1)


def scratch():
    shapes = []
    for _ in range(2):
        shapes += [pltpu.VMEM((TILES, 128, 128), F32)] * len(MODULE_FIELDS)
        shapes += [pltpu.VMEM((128, CELLS), BF16)] * len(FLAT_FIELDS)
        shapes += [
            pltpu.VMEM((512, CELLS), BF16),
            pltpu.VMEM((TILES, 8, 128), F32),
            pltpu.VMEM((TILES, 8, 128), F32),
            pltpu.VMEM((512, 128), BF16),
            pltpu.VMEM((128, 128), BF16),
            pltpu.VMEM((128, 128), BF16),
            pltpu.VMEM((WIDE, WIDE), BF16),
            pltpu.VMEM((WIDE, WIDE), BF16),
            pltpu.VMEM((DEVICES * GRD, 128), F32),
            pltpu.VMEM((DEVICES, GRD, 128), F32),
            pltpu.VMEM((DEVICES * GRD, 128), F32),
        ]
    shapes += [pltpu.VMEM((TILES, 128, 128), F32)] * 4
    shapes += [
        pltpu.VMEM((DEVICES * DBL, 128), F32),
        pltpu.VMEM((WIDE, WIDE), BF16),
        pltpu.VMEM((4, DEVICES, DBL, 128), BF16),
        pltpu.VMEM((4, DEVICES, DBL, 128), BF16),
        pltpu.VMEM((4, DEVICES, SGL, 128), BF16),
        pltpu.VMEM((4, DEVICES, SGL, 128), BF16),
        pltpu.SemaphoreType.DMA((12,)),
        pltpu.SemaphoreType.DMA((12,)),
    ]
    return shapes


def local(*args):
    vmem = pl.BlockSpec(memory_space=pltpu.VMEM)
    pair = jax.ShapeDtypeStruct((BI, BK, C), F32)
    square = jax.ShapeDtypeStruct((C, C), F32)
    proj = jax.ShapeDtypeStruct((C, 4 * C), F32)
    return pl.pallas_call(
        kernel,
        out_shape=(pair, pair, proj, square, square, proj, square, square),
        in_specs=[vmem] * 8,
        out_specs=(vmem,) * 8,
        scratch_shapes=scratch(),
        compiler_params=pltpu.CompilerParams(
            has_side_effects=True, collective_id=0, vmem_limit_bytes=58 * 2**20
        ),
        name="triangles",
    )(*args)


def solution(mesh):
    specs = (P("row", "col", None), P("row", "col", None), P(), P(), P(), P(), P(), P())
    return jax.shard_map(local, mesh=mesh, in_specs=specs, out_specs=specs, check_vma=False)
```

time: 821 us -> 164 us (0.20)
  waiting for transfers between devices: 617 us -> 0 us
  Pallas kernels: 0 us -> 155 us
  local copies, waits for them, and re-layouts: 92.8 us -> 7.78 us
  matrix products: 72 us -> 0 us
  other arithmetic: 21.9 us -> 0 us
  between operations: 14.6 us -> 0.66 us
    reduce_scatter x4 -> x0, waiting for transfers between devices: 240 us -> none  [the longest x1 81.3 us: local(): lax.psum_scatter(jnp.einsum('kih,kjh->ijh', block, right_c, preferred_ele...]
    all_gather x4 -> x0, waiting for transfers between devices: 229 us -> none  [the longest x1 60.1 us: local(): right_cols = lax.all_gather(right_a, 'row', axis=0, tiled=True)]
    pallas_call x0 -> x1, Pallas kernels: none -> 155 us  [local(): pl.pallas_call(kernel, out_shape=(pair, pair, proj, square, square, proj,...]
    psum x1 -> x0, waiting for transfers between devices: 147 us -> none  [local(): lax.psum((dproj_out, dgate_out, dlift_out, dproj_inc, dgate_inc, dlift_in...]
    dot_general x24 -> x0, matrix products: 72 us -> none  [the longest x12 12.9 us: flat_dot(): jnp.dot(first.reshape(-1, first.shape[-1]), matrix, preferred_element_typ...]
    all_gather x4 -> x0, local copies, waits for them, and re-layouts: 44.9 us -> none  [the longest x1 17.8 us: local(): tri_cols = lax.all_gather(grad_tri_c, 'row', axis=0, tiled=True)]
    dot_general x4 -> x0, local copies, waits for them, and re-layouts: 17.6 us -> none  [the longest x1 7.57 us: local(): jnp.einsum('ijh,ikh->jkh', block, left_a, preferred_element_type=jnp.floa...]
    convert_element_type x5 -> x0, local copies, waits for them, and re-layouts: 15.7 us -> none  [the longest x1 7.57 us: local(): jnp.einsum('kih,kjh->ijh', block, right_c, preferred_element_type=jnp.flo...]
  transfers between devices with their start and end apart: 9 -> 0, of which waited for: 9 -> 0; matrix products, arithmetic and copies ran while one was open for 4% -> 0% of each run, Pallas kernels for 0% -> 0%
where the time goes in v1:
time: 164 us; the launch traced here: 163 us
  Pallas kernels  155 us (95%)
  local copies, waits for them, and re-layouts  7.78 us (5%)
    pallas_call x1, Pallas kernels, local(): pl.pallas_call(kernel, out_shape=(pair, pair, proj, square, square, proj,...  155 us
    unnamed x22, local copies, waits for them, and re-layouts  7.78 us

profile of v1, /device:TPU:1, one launch (start us, length us, event | category | flops | bytes accessed | tf_op | source)
XLA Modules:
  0.0 163.2 jit_solution(13271237516490853892)
XLA Ops:
  0.6 154.8 %triangles.1 = (f32[24,48,128]{2,1,0:T(8,128)}, f32[24,48,128]{2,1,0:T(8,128)}, f32[128,512]{1,0:T(8,128)}, f32[128,128]{1,0:T(8,128)}, f32[128,128]{1,0:T(8,128...) custom-call(f32[24,48,128]{2,1,0:T(8,128)} %refs_0_.1, f32[24,48,128]{2,1,0:T(8,128)} %refs_1_.1, ...), custom_call_target="tpu_custom_call" | custom-call | tf_op jit(solution)/shard_map/triangles/pallas_call | solution.py:410
  155.4 0.0 copy-start
  155.5 2.0 %copy.24 = f32[24,48,128]{2,1,0:T(8,128)} copy(f32[24,48,128]{2,1,0:T(8,128)} %get-tuple-element.16) | data formatting | bytes 1179648
  157.4 0.0 copy-done
  157.4 0.0 copy-start.2
  157.4 0.8 copy.25
  158.3 0.3 copy-done.2
  158.5 0.0 copy-start.6
  158.5 0.0 copy-start.1
  158.5 0.7 copy.26
  159.2 0.2 copy-done.6
  159.4 0.0 copy-start.5
  159.4 0.6 copy.27
  160.0 0.2 copy-done.5
  160.3 0.6 copy.28
  160.9 0.0 copy-done.1
  160.9 0.0 copy-start.4
  160.9 0.7 copy.29
  161.6 0.2 copy-done.4
  161.8 0.0 copy-start.3
  161.8 0.6 copy.30
  162.4 0.2 copy-done.3
  162.6 0.6 copy.31
Async XLA Ops:
  155.4 2.0 %copy-start = (f32[24,48,128]{2,1,0:T(8,128)S(1)}, f32[24,48,128]{2,1,0:T(8,128)}, u32[]{:S(2)}) copy-start(f32[24,48,128]{2,1,0:T(8,128)} %get-tuple-element.17) | copy-start | bytes 1769476
  157.4 1.1 copy-start.2
  158.5 0.9 copy-start.6
  158.5 2.4 %copy-start.1 = (f32[128,512]{1,0:T(8,128)S(1)}, f32[128,512]{1,0:T(8,128)}, u32[]{:S(2)}) copy-start(f32[128,512]{1,0:T(8,128)} %get-tuple-element.21) | copy-start | bytes 786436
  159.4 0.9 copy-start.5
  160.9 0.9 copy-start.4
  161.8 0.9 copy-start.3

commit v2 on v1

--- a/solution.py
+++ b/solution.py
@@ -18,7 +18,13 @@
 SLOT = 64
 WIDE = COLS * SLOT
 CELLS = TILES * 128
-DBL, SGL, GRD = 24, 16, 8
+DBL, SGL = 24, 16
+GRD, TAIL = 8, 4
+OFFSETS = sorted(
+    ((dx, dy, dz, dc) for dx in range(4) for dy in range(4) for dz in range(4) for dc in range(2)),
+    key=lambda o: -sum(min(v, 4 - v) for v in o[:3]),
+)
+OFFSETS.remove((0, 0, 0, 0))
 
 MODULE_FIELDS = ("n", "s1", "p2", "s3", "p4", "gate", "u", "lifted")
 FLAT_FIELDS = ("nb", "ub", "gl", "gg")
@@ -48,30 +54,27 @@
 
     def module(wp, wg, wl):
         m = types.SimpleNamespace(wp=wp, wg=wg, wl=wl)
-        for name in MODULE_FIELDS + FLAT_FIELDS + ("gp", "r", "ur", "wpt", "wgt", "wlt", "ml", "mr", "ws", "wr", "wa"):
+        for name in MODULE_FIELDS + FLAT_FIELDS + ("gp", "r", "ur", "wpt", "wgt", "wlt", "ml", "mr"):
             setattr(m, name, next(it))
         return m
 
     out, inc = module(wp_o, wg_o, wl_o), module(wp_i, wg_i, wl_i)
-    xt, ct, mt, gt, stage, gmat, snd_d, rec_d, snd_s, rec_s, ssem, rsem = it
+    xt, ct, mt, gt, stage, gmat, snd_d, rec_d, snd_s, rec_s = (next(it) for _ in range(10))
+    ws, ga, gb, ssem, rsem = next(it), (next(it), next(it), next(it)), (next(it), next(it), next(it)), next(it), next(it)
 
     row, col = lax.axis_index("row"), lax.axis_index("col")
     me = row * COLS + col
-    cols = [lax.rem(col + b, COLS) for b in range(COLS)]
+    x = row // 8 * 2 + lax.rem(col, 2)
+    xs = [lax.rem(x + d, 4) for d in range(4)]
+    row_x = [v // 2 * 8 for v in xs]
+    col_x = [lax.rem(v, 2) for v in xs]
+    row_z = [lax.rem(lax.rem(row, 8) // 2 + d, 4) * 2 for d in range(4)]
+    col_y = [lax.rem(col // 2 + d, 4) * 2 for d in range(4)]
+    row_c = [lax.rem(row + d, 2) for d in range(2)]
 
     def peers(visit):
-        def step(a, carry):
-            rr = lax.rem(row + a, ROWS)
-            for b in range(COLS):
-                if b:
-                    visit(rr, cols[b])
-                else:
-                    @pl.when(a > 0)
-                    def _():
-                        visit(rr, cols[0])
-            return carry
-
-        lax.fori_loop(0, ROWS, step, 0)
+        for dx, dy, dz, dc in OFFSETS:
+            visit(row_x[dx] + row_z[dz] + row_c[dc], col_y[dy] + col_x[dx])
 
     barrier = pltpu.get_barrier_semaphore()
     peers(lambda rr, cc: pl.semaphore_signal(barrier, inc=1, device_id=(rr, cc), device_id_type=MESH))
@@ -88,17 +91,24 @@
     def arrive(ref, k):
         drain(ref, rsem, k)
 
+    def piece(p, size):
+        return stage[pl.ds(pl.multiple_of(p * size, 8), size), :]
+
+    def put(ref, p, value):
+        if ref.shape[1:] == (3, 4, 128):
+            for j in range(3):
+                ref[p, j] = value[4 * j : 4 * j + 4].astype(BF16)
+        else:
+            ref[p] = value.astype(BF16)
+
     def send_staged(snd, dst, k, size):
-        def piece(p):
-            return stage[pl.ds(pl.multiple_of(p * size, 8), size), :].astype(BF16)
-
         def visit(rr, cc):
             p = rr * COLS + cc
-            snd[p] = piece(p)
+            put(snd, p, piece(p, size))
             start(snd.at[p], dst.at[me], k, rr, cc)
 
         peers(visit)
-        dst[me] = piece(me)
+        put(dst, me, piece(me, size))
 
     def send_ready(snd, dst, k):
         peers(lambda rr, cc: start(snd.at[rr * COLS + cc], dst.at[me], k, rr, cc))
@@ -108,13 +118,18 @@
         def step(a, carry):
             for b in range(COLS):
                 p = a * COLS + b
-                stage[pl.ds(pl.multiple_of(p * size, 8), size), :] = rec[p].astype(F32)
+                at = pl.multiple_of(p * size, 8)
+                if rec.shape[1:] == (3, 4, 128):
+                    for j in range(3):
+                        stage[pl.ds(at + 4 * j, 4), :] = rec[p, j].astype(F32)
+                else:
+                    stage[pl.ds(at, size), :] = rec[p].astype(F32)
             return carry
 
         lax.fori_loop(0, ROWS, step, 0)
 
     def tiles(body):
-        lax.fori_loop(0, TILES, lambda t, carry: (body(t), carry)[1], 0)
+        lax.fori_loop(0, TILES, lambda t, carry: (body(t), carry)[1], 0, unroll=4)
 
     low = lax.broadcasted_iota(jnp.int32, (BI, 128), 1) < SLOT
     top = lax.broadcasted_iota(jnp.int32, (BI, 128), 0) < TILES
@@ -147,13 +162,15 @@
         lax.fori_loop(0, ROWS // 2, step, 0)
 
     def assemble_single(rec, whole):
+        unpack(rec, SGL)
+
         def step(r2, carry):
             at = pl.ds(pl.multiple_of(r2 * SLOT, SLOT), SLOT)
             for m in range(COLS // 2):
                 ls = []
                 for s in range(2):
                     p = (2 * r2 + s) * COLS + 2 * m
-                    a, b = (jnp.concatenate([rec[q].astype(F32), gap8], axis=0) for q in (p, p + 1))
+                    a, b = (jnp.concatenate([piece(q, SGL), gap8], axis=0) for q in (p, p + 1))
                     o0, o1 = halves(a, b)
                     ls.append(jnp.where(top, o0, swap_rows(o1)))
                 whole[at, m * 128 : (m + 1) * 128] = jnp.concatenate(ls + [gap16], axis=0).astype(BF16)
@@ -175,8 +192,8 @@
                     p = (4 * q + s4) * COLS + 2 * m
                     ms = [cut(b[lo : lo + BI, m * 128 : (m + 1) * 128], j) for j, b in enumerate(blocks)]
                     if len(ms) == 1:
-                        snd[p] = ms[0][0][:SGL].astype(BF16)
-                        snd[p + 1] = ms[0][1][:SGL].astype(BF16)
+                        put(snd, p, ms[0][0])
+                        put(snd, p + 1, ms[0][1])
                     else:
                         snd[p] = jnp.where(top, ms[0][0], ms[1][0]).astype(BF16)
                         snd[p + 1] = jnp.where(top, ms[0][1], ms[1][1]).astype(BF16)
@@ -250,45 +267,49 @@
         gn = dot(m.wp[...], m.gp[:, lanes(t)]) + dot(m.wg[...], m.gg[:, lanes(t)])
         return g + norm_back(gn, m.n[t], m.r[t][0:1])
 
-    def weight_rows(m, j, value):
-        m.ws[pl.ds(j, 128, stride=GRD), :] = value
-
-    def small_grads(m):
-        weight_rows(m, 4, dot(m.nb[...], m.gg[...], 1, 1))
-        weight_rows(m, 5, dot(m.ub[...], m.gl[...], 1, 1))
-
-    def proj_grads(m):
+    def rows_of_grads(j, size, value):
+        ws[pl.ds(j, 128, stride=size), :] = value
+
+    def proj_grads(m, size):
         for j in range(4):
-            weight_rows(m, j, dot(m.nb[...], m.gp[j * 128 : (j + 1) * 128, :], 1, 1))
-
-    def part(ref, p):
-        return ref.at[pl.ds(pl.multiple_of(p * GRD, GRD), GRD)]
-
-    def scatter_grads(m, k):
-        peers(lambda rr, cc: start(part(m.ws, rr * COLS + cc), m.wr.at[me], k, rr, cc))
-        m.wr[me] = m.ws[pl.ds(pl.multiple_of(me * GRD, GRD), GRD), :]
-
-    def gather_grads(m, k):
-        arrive(m.wr, k)
-        total = lax.fori_loop(
-            0, ROWS, lambda a, acc: acc + jnp.sum(m.wr[pl.ds(a * COLS, COLS)], axis=0), jnp.zeros((GRD, 128), F32)
-        )
-        m.wa[pl.ds(pl.multiple_of(me * GRD, GRD), GRD), :] = total
-        peers(lambda rr, cc: start(part(m.wa, me), part(m.wa, me), k + 1, rr, cc))
-
-    def write_grads(m, k, dp, dg, dl):
-        span = m.wa.at[pl.ds(0, (DEVICES - 1) * GRD)]
-        pltpu.make_async_copy(span, span, rsem.at[k + 1]).wait()
-        for j in range(4):
-            dp[:, j * 128 : (j + 1) * 128] = m.wa[pl.ds(j, 128, stride=GRD), :]
-        dg[...] = m.wa[pl.ds(4, 128, stride=GRD), :]
-        dl[...] = m.wa[pl.ds(5, 128, stride=GRD), :]
+            rows_of_grads(j, size, dot(m.nb[...], m.gp[j * 128 : (j + 1) * 128, :], 1, 1))
+
+    def pack_grads(snd, size):
+        def step(a, carry):
+            for b in range(COLS):
+                at = pl.multiple_of(a * (COLS * size), 8) + b * size
+                snd[a * COLS + b] = ws[pl.ds(at, size), :].astype(BF16)
+            return carry
+
+        lax.fori_loop(0, ROWS, step, 0)
+
+    def sum_grads(rec, whole, size):
+        whole[me] = lax.fori_loop(
+            0,
+            ROWS,
+            lambda a, acc: acc + jnp.sum(rec[pl.ds(a * COLS, COLS)].astype(F32), axis=0),
+            jnp.zeros((size, 128), F32),
+        ).astype(BF16)
+
+    def spread_grads(whole, k):
+        peers(lambda rr, cc: start(whole.at[me], whole.at[me], k, rr, cc))
+
+    def unpack_grads(whole, size):
+        def step(a, carry):
+            for b in range(COLS):
+                at = pl.multiple_of(a * (COLS * size), 8) + b * size
+                ws[pl.ds(at, size), :] = whole[a * COLS + b].astype(F32)
+            return carry
+
+        lax.fori_loop(0, ROWS, step, 0)
+
+    def write_rows(j, size, dst):
+        dst[...] = ws[pl.ds(j, 128, stride=size), :]
 
     for m in (out, inc):
         m.wpt[...] = m.wp[...].T
         m.wgt[...] = m.wg[...].T
         m.wlt[...] = m.wl[...].T
-        m.ws[...] = jnp.zeros(m.ws.shape, F32)
     into_tiles(pair, xt)
     tiles(lambda t: project(t, xt[t], out))
     pl.semaphore_wait(barrier, DEVICES - 1)
@@ -328,7 +349,6 @@
         lambda at: [dot(inc.mr[at, :], gmat[...], 1, 1), dot(inc.ml[at, :], gmat[...], 1, 0)], snd_d.at[2]
     )
     send_ready(snd_d.at[2], rec_d.at[2], 5)
-    small_grads(inc)
     arrive(rec_d.at[2], 5)
     unpack(rec_d.at[2], DBL)
 
@@ -341,33 +361,50 @@
 
     tiles(grad_middle_tile)
     send_staged(snd_s.at[3], rec_s.at[3], 6, SGL)
-    proj_grads(inc)
-    scatter_grads(inc, 8)
+    proj_grads(inc, GRD)
+    rows_of_grads(4, GRD, dot(inc.nb[...], inc.gg[...], 1, 1))
+    rows_of_grads(5, GRD, dot(inc.ub[...], inc.gl[...], 1, 1))
+    rows_of_grads(6, GRD, dot(out.nb[...], out.gg[...], 1, 1))
+    rows_of_grads(7, GRD, dot(out.ub[...], out.gl[...], 1, 1))
+    pack_grads(ga[0], GRD)
     arrive(rec_s.at[3], 6)
+    send_ready(ga[0], ga[1], 8)
     assemble_single(rec_s.at[3], gmat)
     split_rows(
         lambda at: [dot(gmat[at, :], out.mr[...], 1, 0), dot(gmat[:, at], out.ml[...], 0, 0)], snd_d.at[3]
     )
     send_ready(snd_d.at[3], rec_d.at[3], 7)
-    small_grads(out)
-    gather_grads(inc, 8)
+    arrive(ga[1], 8)
+    sum_grads(ga[1], ga[2], GRD)
     arrive(rec_d.at[3], 7)
+    spread_grads(ga[2], 9)
     unpack(rec_d.at[3], DBL)
     tiles(lambda t: pre_back(t, out))
-    proj_grads(out)
-    scatter_grads(out, 10)
+    proj_grads(out, TAIL)
+    pack_grads(gb[0], TAIL)
+    send_ready(gb[0], gb[1], 10)
     tiles(lambda t: out_tile(t, tail_back(t, gt[t], out), grad))
-    write_grads(inc, 8, dpi, dgi, dli)
-    gather_grads(out, 10)
-    write_grads(out, 10, dpo, dgo, dlo)
+    arrive(gb[1], 10)
+    sum_grads(gb[1], gb[2], TAIL)
+    spread_grads(gb[2], 11)
+    arrive(ga[2], 9)
+    unpack_grads(ga[2], GRD)
+    for j in range(4):
+        write_rows(j, GRD, dpi.at[:, j * 128 : (j + 1) * 128])
+    for j, dst in ((4, dgi), (5, dli), (6, dgo), (7, dlo)):
+        write_rows(j, GRD, dst)
+    arrive(gb[2], 11)
+    unpack_grads(gb[2], TAIL)
+    for j in range(4):
+        write_rows(j, TAIL, dpo.at[:, j * 128 : (j + 1) * 128])
 
     for j, k in enumerate((0, 2, 5, 7)):
         drain(snd_d.at[j], ssem, k)
     for j, k in enumerate((1, 3, 4, 6)):
         drain(snd_s.at[j], ssem, k)
-    for m, k in ((inc, 8), (out, 10)):
-        drain(m.wr, ssem, k)
-        drain(m.wr, ssem, k + 1)
+    for g, k in ((ga, 8), (gb, 10)):
+        drain(g[0], ssem, k)
+        drain(g[2], ssem, k + 1)
 
 
 def scratch():
@@ -384,9 +421,6 @@
             pltpu.VMEM((128, 128), BF16),
             pltpu.VMEM((WIDE, WIDE), BF16),
             pltpu.VMEM((WIDE, WIDE), BF16),
-            pltpu.VMEM((DEVICES * GRD, 128), F32),
-            pltpu.VMEM((DEVICES, GRD, 128), F32),
-            pltpu.VMEM((DEVICES * GRD, 128), F32),
         ]
     shapes += [pltpu.VMEM((TILES, 128, 128), F32)] * 4
     shapes += [
@@ -394,8 +428,13 @@
         pltpu.VMEM((WIDE, WIDE), BF16),
         pltpu.VMEM((4, DEVICES, DBL, 128), BF16),
         pltpu.VMEM((4, DEVICES, DBL, 128), BF16),
-        pltpu.VMEM((4, DEVICES, SGL, 128), BF16),
-        pltpu.VMEM((4, DEVICES, SGL, 128), BF16),
+        pltpu.VMEM((4, DEVICES, 3, 4, 128), BF16),
+        pltpu.VMEM((4, DEVICES, 3, 4, 128), BF16),
+        pltpu.VMEM((DEVICES * GRD, 128), F32),
+    ]
+    shapes += [pltpu.VMEM((DEVICES, GRD, 128), BF16)] * 3
+    shapes += [pltpu.VMEM((DEVICES, TAIL, 128), BF16)] * 3
+    shapes += [
         pltpu.SemaphoreType.DMA((12,)),
         pltpu.SemaphoreType.DMA((12,)),
     ]

time: 164 us -> 133 us (0.81)
  Pallas kernels: 155 us -> 125 us
    pallas_call x1, Pallas kernels: 155 us -> 125 us  [local(): pl.pallas_call(kernel, out_shape=(pair, pair, proj, square, square, proj,...]
where the time goes in v2:
time: 133 us
  Pallas kernels  125 us (94%)
  local copies, waits for them, and re-layouts  7.78 us (6%)
    pallas_call x1, Pallas kernels, local(): pl.pallas_call(kernel, out_shape=(pair, pair, proj, square, square, proj,...  125 us
    unnamed x22, local copies, waits for them, and re-layouts  7.78 us

profile of v2, /device:TPU:1, one launch (start us, length us, event | category | flops | bytes accessed | tf_op | source)
XLA Modules:
  0.0 133.1 jit_solution(12407766609452463544)
XLA Ops:
  0.6 124.6 %triangles.1 = (f32[24,48,128]{2,1,0:T(8,128)}, f32[24,48,128]{2,1,0:T(8,128)}, f32[128,512]{1,0:T(8,128)}, f32[128,128]{1,0:T(8,128)}, f32[128,128]{1,0:T(8,128...) custom-call(f32[24,48,128]{2,1,0:T(8,128)} %refs_0_.1, f32[24,48,128]{2,1,0:T(8,128)} %refs_1_.1, ...), custom_call_target="tpu_custom_call" | custom-call | tf_op jit(solution)/shard_map/triangles/pallas_call | solution.py:449
  125.3 0.0 copy-start
  125.3 2.0 %copy.24 = f32[24,48,128]{2,1,0:T(8,128)} copy(f32[24,48,128]{2,1,0:T(8,128)} %get-tuple-element.16) | data formatting | bytes 1179648
  127.3 0.0 copy-done
  127.3 0.0 copy-start.2
  127.3 0.8 copy.25
  128.1 0.3 copy-done.2
  128.4 0.0 copy-start.6
  128.4 0.0 copy-start.1
  128.4 0.7 copy.26
  129.1 0.2 copy-done.6
  129.2 0.0 copy-start.5
  129.2 0.6 copy.27
  129.8 0.2 copy-done.5
  130.1 0.6 copy.28
  130.7 0.0 copy-done.1
  130.7 0.0 copy-start.4
  130.7 0.7 copy.29
  131.4 0.2 copy-done.4
  131.6 0.0 copy-start.3
  131.6 0.6 copy.30
  132.2 0.2 copy-done.3
  132.4 0.6 copy.31
Async XLA Ops:
  125.3 2.0 %copy-start = (f32[24,48,128]{2,1,0:T(8,128)S(1)}, f32[24,48,128]{2,1,0:T(8,128)}, u32[]{:S(2)}) copy-start(f32[24,48,128]{2,1,0:T(8,128)} %get-tuple-element.17) | copy-start | bytes 1769476
  127.3 1.1 copy-start.2
  128.4 0.9 copy-start.6
  128.4 2.4 %copy-start.1 = (f32[128,512]{1,0:T(8,128)S(1)}, f32[128,512]{1,0:T(8,128)}, u32[]{:S(2)}) copy-start(f32[128,512]{1,0:T(8,128)} %get-tuple-element.21) | copy-start | bytes 786436
  129.2 0.9 copy-start.5
  130.7 0.9 copy-start.4
  131.6 0.9 copy-start.3

commit v3 on v2

v3 whole, which is shorter than its diff:
```python
import types

import jax
import jax.numpy as jnp
from jax import lax
from jax.experimental import pallas as pl
from jax.experimental.pallas import tpu as pltpu
from jax.sharding import PartitionSpec as P

F32 = jnp.float32
BF16 = jnp.bfloat16
EPSILON = 1e-05
MESH = pl.DeviceIdType.MESH

ROWS, COLS, DEVICES = 16, 8, 128
BI, BK, C = 24, 48, 128
TILES = 12
SLOT = 64
WIDE = COLS * SLOT
CELLS = TILES * 128
SGL = 16
GRD, TAIL = 8, 4
OFFSETS = sorted(
    ((dx, dy, dz, dc) for dx in range(4) for dy in range(4) for dz in range(4) for dc in range(2)),
    key=lambda o: -sum(min(v, 4 - v) for v in o[:3]),
)
OFFSETS.remove((0, 0, 0, 0))

MODULE_FIELDS = ("n", "s1", "p2", "s3", "p4", "gate", "u", "lifted")
FLAT_FIELDS = ("nb", "ub", "gl", "gg")


def dot(a, b, ca=1, cb=0):
    return lax.dot_general(a, b, (((ca,), (cb,)), ((), ())), preferred_element_type=F32)


def norm(p):
    d = p - jnp.mean(p, axis=0, keepdims=True)
    r = lax.rsqrt(jnp.mean(d * d, axis=0, keepdims=True) + EPSILON)
    return d * r, r


def norm_back(q, n, r):
    return (q - jnp.mean(q, axis=0, keepdims=True) - n * jnp.mean(q * n, axis=0, keepdims=True)) * r


def lanes(t):
    return pl.ds(pl.multiple_of(t * 128, 128), 128)


def kernel(*refs):
    (pair, cot, wp_o, wg_o, wl_o, wp_i, wg_i, wl_i, res, grad, dpo, dgo, dlo, dpi, dgi, dli) = refs[:16]
    it = iter(refs[16:])

    def module(wp, wg, wl):
        m = types.SimpleNamespace(wp=wp, wg=wg, wl=wl)
        for name in MODULE_FIELDS + FLAT_FIELDS + ("gp", "r", "ur", "wpt", "wgt", "wlt", "ml", "mr"):
            setattr(m, name, next(it))
        return m

    out, inc = module(wp_o, wg_o, wl_o), module(wp_i, wg_i, wl_i)
    xt, ct, mt, gt, stage, gmat, snd, rec, res_v, grad_v = (next(it) for _ in range(10))
    ws, ga, gb, ssem, rsem = next(it), (next(it), next(it), next(it)), (next(it), next(it), next(it)), next(it), next(it)
    osem = next(it)

    row, col = lax.axis_index("row"), lax.axis_index("col")
    me = row * COLS + col
    x = row // 8 * 2 + lax.rem(col, 2)
    xs = [lax.rem(x + d, 4) for d in range(4)]
    row_x = [v // 2 * 8 for v in xs]
    col_x = [lax.rem(v, 2) for v in xs]
    row_z = [lax.rem(lax.rem(row, 8) // 2 + d, 4) * 2 for d in range(4)]
    col_y = [lax.rem(col // 2 + d, 4) * 2 for d in range(4)]
    row_c = [lax.rem(row + d, 2) for d in range(2)]

    def peers(visit):
        for dx, dy, dz, dc in OFFSETS:
            visit(row_x[dx] + row_z[dz] + row_c[dc], col_y[dy] + col_x[dx])

    barrier = pltpu.get_barrier_semaphore()
    peers(lambda rr, cc: pl.semaphore_signal(barrier, inc=1, device_id=(rr, cc), device_id_type=MESH))

    def start(src, dst, k, rr, cc):
        pltpu.make_async_remote_copy(
            src, dst, ssem.at[k], rsem.at[k], device_id=(rr, cc), device_id_type=MESH
        ).start()

    def drain(ref, sem, k):
        span = ref.at[pl.ds(0, DEVICES - 1)]
        pltpu.make_async_copy(span, span, sem.at[k]).wait()

    def arrive(ref, k):
        drain(ref, rsem, k)

    def piece(p):
        return stage[pl.ds(pl.multiple_of(p * SGL, SGL), SGL), :]

    def put(ref, p, value):
        for j in range(3):
            ref[p, j] = value[4 * j : 4 * j + 4].astype(BF16)

    def send_staged(k):
        def visit(rr, cc):
            p = rr * COLS + cc
            put(snd.at[k], p, piece(p))
            start(snd.at[k, p], rec.at[k, me], k, rr, cc)

        peers(visit)
        put(rec.at[k], me, piece(me))

    def send_ready(src, dst, k):
        peers(lambda rr, cc: start(src.at[rr * COLS + cc], dst.at[me], k, rr, cc))
        dst[me] = src[me]

    def unpack(k):
        def step(a, carry):
            for b in range(COLS):
                p = a * COLS + b
                for j in range(3):
                    stage[pl.ds(pl.multiple_of(p * SGL, SGL) + 4 * j, 4), :] = rec[k, p, j].astype(F32)
            return carry

        lax.fori_loop(0, ROWS, step, 0)

    def tiles(body):
        lax.fori_loop(0, TILES, lambda t, carry: (body(t), carry)[1], 0, unroll=4)

    low = lax.broadcasted_iota(jnp.int32, (BI, 128), 1) < SLOT
    top = lax.broadcasted_iota(jnp.int32, (BI, 128), 0) < TILES
    gap8 = jnp.zeros((8, 128), F32)
    gap16 = jnp.zeros((16, 128), F32)

    def swap_lanes(a):
        return pltpu.roll(a, SLOT, 1)

    def swap_rows(a):
        return pltpu.roll(a, TILES, 0)

    def halves(a, b):
        return jnp.where(low, a, swap_lanes(b)), jnp.where(low, swap_lanes(a), b)

    def assemble(k, whole):
        unpack(k)

        def step(r2, carry):
            at = pl.ds(pl.multiple_of(r2 * SLOT, SLOT), SLOT)
            for m in range(COLS // 2):
                ls = []
                for s in range(2):
                    p = (2 * r2 + s) * COLS + 2 * m
                    a, b = (jnp.concatenate([piece(q), gap8], axis=0) for q in (p, p + 1))
                    o0, o1 = halves(a, b)
                    ls.append(jnp.where(top, o0, swap_rows(o1)))
                whole[at, m * 128 : (m + 1) * 128] = jnp.concatenate(ls + [gap16], axis=0).astype(BF16)
            return carry

        lax.fori_loop(0, ROWS // 2, step, 0)

    half = row // 4

    def send_rows(rows_of, k):
        def step(i, carry):
            q = lax.rem(half // 2 + 1 + i // 2, 2) * 2 + lax.rem(half + 1 + i, 2)
            block = rows_of(pl.ds(pl.multiple_of(q * 128, 128), 128))
            for s4 in range(4):
                lo = SLOT * (s4 // 2) + BI * (s4 % 2)
                for m in range(COLS // 2):
                    p = (4 * q + s4) * COLS + 2 * m
                    first = block[lo : lo + BI, m * 128 : (m + 1) * 128]
                    a, b = halves(first, swap_rows(first))
                    put(snd.at[k], p, a)
                    put(snd.at[k], p + 1, b)
            for d in (2, 1, 3, 0):
                for s4 in range(4):
                    for x_lo in range(2):
                        rr, cc = 4 * q + s4, col_y[d] + x_lo
                        p = rr * COLS + cc
                        if d:
                            start(snd.at[k, p], rec.at[k, me], k, rr, cc)
                        else:
                            @pl.when(p != me)
                            def _():
                                start(snd.at[k, p], rec.at[k, me], k, rr, cc)
            return carry

        lax.fori_loop(0, WIDE // 128, step, 0)
        rec[k, me] = snd[k, me]

    def into_tiles(src, dst):
        def body(t):
            rows = jnp.concatenate([src[t], gap16, src[TILES + t], gap16], axis=0)
            dst[t] = rows.T

        tiles(body)

    def out_tile(t, value, dst):
        back = value.T
        dst[t] = back[:BK]
        dst[TILES + t] = back[SLOT : SLOT + BK]

    def strided(t):
        return stage[pl.ds(t, 128, stride=SGL), :]

    def put_strided(t, value):
        stage[pl.ds(t, 128, stride=SGL), :] = value

    def project_left(t, x, m):
        n, r = norm(x)
        nb = n.astype(BF16)
        m.n[t] = n
        m.r[t] = jnp.broadcast_to(r, (8, 128))
        m.nb[:, lanes(t)] = nb
        s1 = jax.nn.sigmoid(dot(m.wpt[0:128], nb))
        p2 = dot(m.wpt[128:256], nb)
        m.s1[t] = s1
        m.p2[t] = p2
        put_strided(t, s1 * p2)

    def project_right(t, m):
        nb = m.nb[:, lanes(t)]
        s3 = jax.nn.sigmoid(dot(m.wpt[256:384], nb))
        p4 = dot(m.wpt[384:512], nb)
        m.s3[t] = s3
        m.p4[t] = p4
        put_strided(t, s3 * p4)

    def project_gate(t, m):
        m.gate[t] = jax.nn.sigmoid(dot(m.wgt[...], m.nb[:, lanes(t)]))

    def finish(t, tri, base, m):
        u, r = norm(tri)
        ub = u.astype(BF16)
        m.u[t] = u
        m.ur[t] = jnp.broadcast_to(r, (8, 128))
        m.ub[:, lanes(t)] = ub
        lifted = dot(m.wlt[...], ub)
        m.lifted[t] = lifted
        return base + m.gate[t] * lifted

    def head_back(t, g, m):
        gate = m.gate[t]
        through = g * gate
        gl = through.astype(BF16)
        m.gl[:, lanes(t)] = gl
        m.gg[:, lanes(t)] = (through * m.lifted[t] * (1.0 - gate)).astype(BF16)
        gunit = dot(m.wl[...], gl)
        put_strided(t, norm_back(gunit, m.u[t], m.ur[t][0:1]))

    def pre_back_left(t, m):
        s1 = m.s1[t]
        a = strided(t) * s1
        m.gp[0:128, lanes(t)] = (a * m.p2[t] * (1.0 - s1)).astype(BF16)
        m.gp[128:256, lanes(t)] = a.astype(BF16)

    def pre_back_right(t, m):
        s3 = m.s3[t]
        b = strided(t) * s3
        m.gp[256:384, lanes(t)] = (b * m.p4[t] * (1.0 - s3)).astype(BF16)
        m.gp[384:512, lanes(t)] = b.astype(BF16)

    def tail_back(t, g, m):
        gn = dot(m.wp[...], m.gp[:, lanes(t)]) + dot(m.wg[...], m.gg[:, lanes(t)])
        return g + norm_back(gn, m.n[t], m.r[t][0:1])

    def rows_of_grads(j, size, value):
        ws[pl.ds(j, 128, stride=size), :] = value

    def proj_grads(m, size):
        for j in range(4):
            rows_of_grads(j, size, dot(m.nb[...], m.gp[j * 128 : (j + 1) * 128, :], 1, 1))

    def pack_grads(snd, size):
        def step(a, carry):
            for b in range(COLS):
                at = pl.multiple_of(a * (COLS * size), 8) + b * size
                snd[a * COLS + b] = ws[pl.ds(at, size), :].astype(BF16)
            return carry

        lax.fori_loop(0, ROWS, step, 0)

    def sum_grads(rec, whole, size):
        whole[me] = lax.fori_loop(
            0,
            ROWS,
            lambda a, acc: acc + jnp.sum(rec[pl.ds(a * COLS, COLS)].astype(F32), axis=0),
            jnp.zeros((size, 128), F32),
        ).astype(BF16)

    def spread_grads(whole, k):
        peers(lambda rr, cc: start(whole.at[me], whole.at[me], k, rr, cc))

    def unpack_grads(whole, size):
        def step(a, carry):
            for b in range(COLS):
                at = pl.multiple_of(a * (COLS * size), 8) + b * size
                ws[pl.ds(at, size), :] = whole[a * COLS + b].astype(F32)
            return carry

        lax.fori_loop(0, ROWS, step, 0)

    def write_rows(j, size, dst):
        dst[...] = ws[pl.ds(j, 128, stride=size), :]

    for m in (out, inc):
        m.wpt[...] = m.wp[...].T
        m.wgt[...] = m.wg[...].T
        m.wlt[...] = m.wl[...].T
    into_tiles(pair, xt)
    tiles(lambda t: project_left(t, xt[t], out))
    pl.semaphore_wait(barrier, DEVICES - 1)
    send_staged(0)
    tiles(lambda t: project_right(t, out))
    send_staged(1)
    tiles(lambda t: project_gate(t, out))
    into_tiles(cot, ct)
    arrive(rec.at[0], 0)
    assemble(0, out.ml)
    arrive(rec.at[1], 1)
    assemble(1, out.mr)
    send_rows(lambda at: dot(out.ml[at, :], out.mr[...], 1, 1), 2)
    arrive(rec.at[2], 2)
    unpack(2)

    def middle_tile(t):
        mid = finish(t, strided(t), xt[t], out)
        mt[t] = mid

    tiles(middle_tile)
    tiles(lambda t: project_left(t, mt[t], inc))
    send_staged(3)
    tiles(lambda t: project_right(t, inc))
    send_staged(4)
    tiles(lambda t: project_gate(t, inc))
    arrive(rec.at[3], 3)
    assemble(3, inc.ml)
    arrive(rec.at[4], 4)
    assemble(4, inc.mr)
    send_rows(lambda at: dot(inc.ml[:, at], inc.mr[...], 0, 0), 5)
    arrive(rec.at[5], 5)
    unpack(5)

    def result_tile(t):
        mt[t] = finish(t, strided(t), mt[t], inc)
        head_back(t, ct[t], inc)

    tiles(result_tile)
    send_staged(6)
    tiles(lambda t: out_tile(t, mt[t], res_v))
    res_out = pltpu.make_async_copy(res_v, res, osem.at[0])
    res_out.start()
    arrive(rec.at[6], 6)
    assemble(6, gmat)
    send_rows(lambda at: dot(inc.mr[at, :], gmat[...], 1, 1), 7)
    send_rows(lambda at: dot(inc.ml[at, :], gmat[...], 1, 0), 8)
    arrive(rec.at[7], 7)
    unpack(7)
    tiles(lambda t: pre_back_left(t, inc))
    arrive(rec.at[8], 8)
    unpack(8)
    tiles(lambda t: pre_back_right(t, inc))

    def grad_middle_tile(t):
        g = tail_back(t, ct[t], inc)
        gt[t] = g
        head_back(t, g, out)

    tiles(grad_middle_tile)
    send_staged(9)
    proj_grads(inc, GRD)
    rows_of_grads(4, GRD, dot(inc.nb[...], inc.gg[...], 1, 1))
    rows_of_grads(5, GRD, dot(inc.ub[...], inc.gl[...], 1, 1))
    rows_of_grads(6, GRD, dot(out.nb[...], out.gg[...], 1, 1))
    rows_of_grads(7, GRD, dot(out.ub[...], out.gl[...], 1, 1))
    pack_grads(ga[0], GRD)
    arrive(rec.at[9], 9)
    send_ready(ga[0], ga[1], 12)
    assemble(9, gmat)
    send_rows(lambda at: dot(gmat[at, :], out.mr[...], 1, 0), 10)
    send_rows(lambda at: dot(gmat[:, at], out.ml[...], 0, 0), 11)
    arrive(ga[1], 12)
    sum_grads(ga[1], ga[2], GRD)
    arrive(rec.at[10], 10)
    unpack(10)
    tiles(lambda t: pre_back_left(t, out))
    arrive(rec.at[11], 11)
    spread_grads(ga[2], 13)
    unpack(11)
    tiles(lambda t: pre_back_right(t, out))
    proj_grads(out, TAIL)
    pack_grads(gb[0], TAIL)
    send_ready(gb[0], gb[1], 14)
    tiles(lambda t: out_tile(t, tail_back(t, gt[t], out), grad_v))
    grad_out = pltpu.make_async_copy(grad_v, grad, osem.at[1])
    grad_out.start()
    arrive(gb[1], 14)
    sum_grads(gb[1], gb[2], TAIL)
    spread_grads(gb[2], 15)
    arrive(ga[2], 13)
    unpack_grads(ga[2], GRD)
    for j in range(4):
        write_rows(j, GRD, dpi.at[:, j * 128 : (j + 1) * 128])
    for j, dst in ((4, dgi), (5, dli), (6, dgo), (7, dlo)):
        write_rows(j, GRD, dst)
    arrive(gb[2], 15)
    unpack_grads(gb[2], TAIL)
    for j in range(4):
        write_rows(j, TAIL, dpo.at[:, j * 128 : (j + 1) * 128])

    for k in range(12):
        drain(snd.at[k], ssem, k)
    for g, k in ((ga, 12), (gb, 14)):
        drain(g[0], ssem, k)
        drain(g[2], ssem, k + 1)
    res_out.wait()
    grad_out.wait()


def scratch():
    shapes = []
    for _ in range(2):
        shapes += [pltpu.VMEM((TILES, 128, 128), F32)] * len(MODULE_FIELDS)
        shapes += [pltpu.VMEM((128, CELLS), BF16)] * len(FLAT_FIELDS)
        shapes += [
            pltpu.VMEM((512, CELLS), BF16),
            pltpu.VMEM((TILES, 8, 128), F32),
            pltpu.VMEM((TILES, 8, 128), F32),
            pltpu.VMEM((512, 128), BF16),
            pltpu.VMEM((128, 128), BF16),
            pltpu.VMEM((128, 128), BF16),
            pltpu.VMEM((WIDE, WIDE), BF16),
            pltpu.VMEM((WIDE, WIDE), BF16),
        ]
    shapes += [pltpu.VMEM((TILES, 128, 128), F32)] * 4
    shapes += [
        pltpu.VMEM((DEVICES * SGL, 128), F32),
        pltpu.VMEM((WIDE, WIDE), BF16),
        pltpu.VMEM((12, DEVICES, 3, 4, 128), BF16),
        pltpu.VMEM((12, DEVICES, 3, 4, 128), BF16),
        pltpu.VMEM((BI, BK, C), F32),
        pltpu.VMEM((BI, BK, C), F32),
        pltpu.VMEM((DEVICES * GRD, 128), F32),
    ]
    shapes += [pltpu.VMEM((DEVICES, GRD, 128), BF16)] * 3
    shapes += [pltpu.VMEM((DEVICES, TAIL, 128), BF16)] * 3
    shapes += [
        pltpu.SemaphoreType.DMA((16,)),
        pltpu.SemaphoreType.DMA((16,)),
        pltpu.SemaphoreType.DMA((2,)),
    ]
    return shapes


def publish(*refs):
    src, dst, held, sem_in, sem_out = refs[:8], refs[8:16], refs[16:24], refs[24], refs[25]
    ins = [pltpu.make_async_copy(src[j], held[j], sem_in.at[j]) for j in range(8)]
    outs = [pltpu.make_async_copy(held[j], dst[j], sem_out.at[j]) for j in range(8)]
    for copy in ins:
        copy.start()
    for copy_in, copy_out in zip(ins, outs):
        copy_in.wait()
        copy_out.start()
    for copy in outs:
        copy.wait()


def local(*args):
    vmem = pl.BlockSpec(memory_space=pltpu.VMEM)
    anywhere = pl.BlockSpec(memory_space=pl.ANY)
    pair = jax.ShapeDtypeStruct((BI, BK, C), F32)
    square = jax.ShapeDtypeStruct((C, C), F32)
    proj = jax.ShapeDtypeStruct((C, 4 * C), F32)
    shapes = (pair, pair, proj, square, square, proj, square, square)
    results = pl.pallas_call(
        kernel,
        out_shape=shapes,
        in_specs=[vmem] * 8,
        out_specs=(anywhere,) * 2 + (vmem,) * 6,
        scratch_shapes=scratch(),
        compiler_params=pltpu.CompilerParams(
            has_side_effects=True, collective_id=0, vmem_limit_bytes=58 * 2**20
        ),
        name="triangles",
    )(*args)
    return pl.pallas_call(
        publish,
        out_shape=shapes,
        in_specs=[anywhere] * 8,
        out_specs=(anywhere,) * 8,
        scratch_shapes=[pltpu.VMEM(v.shape, F32) for v in shapes] + [pltpu.SemaphoreType.DMA((8,))] * 2,
        name="publish",
    )(*results)


def solution(mesh):
    specs = (P("row", "col", None), P("row", "col", None), P(), P(), P(), P(), P(), P())
    return jax.shard_map(local, mesh=mesh, in_specs=specs, out_specs=specs, check_vma=False)
```

time: 133 us -> 126 us (0.947)
  local copies, waits for them, and re-layouts: 7.78 us -> 0 us
    unnamed x22 -> x0, local copies, waits for them, and re-layouts: 7.78 us -> none
    pallas_call x1 -> x2, Pallas kernels: 125 us -> 125 us  [the longest x1 123 us: local(): pl.pallas_call(kernel, out_shape=shapes, in_specs=[vmem] * 8, out_specs=(...]
where the time goes in v3:
time: 126 us
  Pallas kernels  125 us (99%)
    pallas_call x1, Pallas kernels, local(): pl.pallas_call(kernel, out_shape=shapes, in_specs=[vmem] * 8, out_specs=(...  123 us

profile of v3, /device:TPU:1, one launch (start us, length us, event | category | flops | bytes accessed | tf_op | source)
XLA Modules:
  0.0 126.2 jit_solution(2455012659105568384)
XLA Ops:
  0.6 123.0 %triangles.1 = (f32[24,48,128]{2,1,0:T(8,128)}, f32[24,48,128]{2,1,0:T(8,128)}, f32[128,512]{1,0:T(8,128)}, f32[128,128]{1,0:T(8,128)}, f32[128,128]{1,0:T(8,128...) custom-call(f32[24,48,128]{2,1,0:T(8,128)} %refs_0_.1, f32[24,48,128]{2,1,0:T(8,128)} %refs_1_.1, ...), custom_call_target="tpu_custom_call" | custom-call | tf_op jit(solution)/shard_map/triangles/pallas_call | solution.py:473
  123.6 2.5 %publish.1 = (f32[24,48,128]{2,1,0:T(8,128)}, f32[24,48,128]{2,1,0:T(8,128)}, f32[128,512]{1,0:T(8,128)}, f32[128,128]{1,0:T(8,128)}, f32[128,128]{1,0:T(8,128)}...) custom-call(f32[24,48,128]{2,1,0:T(8,128)} %get-tuple-element.16.refs_0_, ...), custom_call_target="tpu_custom_call" | custom-call | tf_op jit(solution)/shard_map/publish/pallas_call | solution.py:484

commit v4 on v3

--- a/solution.py
+++ b/solution.py
@@ -49,8 +49,15 @@
 
 
 def kernel(*refs):
-    (pair, cot, wp_o, wg_o, wl_o, wp_i, wg_i, wl_i, res, grad, dpo, dgo, dlo, dpi, dgi, dli) = refs[:16]
-    it = iter(refs[16:])
+    sources, results, taken, isem = refs[:8], refs[8:16], refs[16:24], refs[24]
+    pair, cot, wp_o, wg_o, wl_o, wp_i, wg_i, wl_i = taken
+    it = iter(refs[25:])
+
+    def enter(j):
+        return pltpu.make_async_copy(sources[j], taken[j], isem.at[j])
+
+    for j in (0, 2, 3, 4, 5, 6, 7, 1):
+        enter(j).start()
 
     def module(wp, wg, wl):
         m = types.SimpleNamespace(wp=wp, wg=wg, wl=wl)
@@ -59,9 +66,11 @@
         return m
 
     out, inc = module(wp_o, wg_o, wl_o), module(wp_i, wg_i, wl_i)
-    xt, ct, mt, gt, stage, gmat, snd, rec, res_v, grad_v = (next(it) for _ in range(10))
+    xt, ct, mt, gt, stage, gmat, snd, rec, pg = (next(it) for _ in range(9))
     ws, ga, gb, ssem, rsem = next(it), (next(it), next(it), next(it)), (next(it), next(it), next(it)), next(it), next(it)
     osem = next(it)
+    held = tuple(it)
+    res, grad, dpo, dgo, dlo, dpi, dgi, dli = held
 
     row, col = lax.axis_index("row"), lax.axis_index("col")
     me = row * COLS + col
@@ -88,6 +97,9 @@
     def drain(ref, sem, k):
         span = ref.at[pl.ds(0, DEVICES - 1)]
         pltpu.make_async_copy(span, span, sem.at[k]).wait()
+
+    def leave(j):
+        return pltpu.make_async_copy(held[j], results[j], osem.at[j])
 
     def arrive(ref, k):
         drain(ref, rsem, k)
@@ -251,6 +263,7 @@
         a = strided(t) * s1
         m.gp[0:128, lanes(t)] = (a * m.p2[t] * (1.0 - s1)).astype(BF16)
         m.gp[128:256, lanes(t)] = a.astype(BF16)
+        pg[t] = dot(m.wp[:, 0:256], m.gp[0:256, lanes(t)]) + dot(m.wg[...], m.gg[:, lanes(t)])
 
     def pre_back_right(t, m):
         s3 = m.s3[t]
@@ -259,14 +272,14 @@
         m.gp[384:512, lanes(t)] = b.astype(BF16)
 
     def tail_back(t, g, m):
-        gn = dot(m.wp[...], m.gp[:, lanes(t)]) + dot(m.wg[...], m.gg[:, lanes(t)])
+        gn = pg[t] + dot(m.wp[:, 256:512], m.gp[256:512, lanes(t)])
         return g + norm_back(gn, m.n[t], m.r[t][0:1])
 
     def rows_of_grads(j, size, value):
         ws[pl.ds(j, 128, stride=size), :] = value
 
-    def proj_grads(m, size):
-        for j in range(4):
+    def proj_grads(m, size, columns):
+        for j in columns:
             rows_of_grads(j, size, dot(m.nb[...], m.gp[j * 128 : (j + 1) * 128, :], 1, 1))
 
     def pack_grads(snd, size):
@@ -301,18 +314,25 @@
     def write_rows(j, size, dst):
         dst[...] = ws[pl.ds(j, 128, stride=size), :]
 
-    for m in (out, inc):
+    def turn(m, first):
+        for j in range(first, first + 3):
+            enter(j).wait()
         m.wpt[...] = m.wp[...].T
         m.wgt[...] = m.wg[...].T
         m.wlt[...] = m.wl[...].T
+
+    enter(0).wait()
     into_tiles(pair, xt)
+    turn(out, 2)
     tiles(lambda t: project_left(t, xt[t], out))
     pl.semaphore_wait(barrier, DEVICES - 1)
     send_staged(0)
     tiles(lambda t: project_right(t, out))
     send_staged(1)
     tiles(lambda t: project_gate(t, out))
+    enter(1).wait()
     into_tiles(cot, ct)
+    turn(inc, 5)
     arrive(rec.at[0], 0)
     assemble(0, out.ml)
     arrive(rec.at[1], 1)
@@ -345,9 +365,8 @@
 
     tiles(result_tile)
     send_staged(6)
-    tiles(lambda t: out_tile(t, mt[t], res_v))
-    res_out = pltpu.make_async_copy(res_v, res, osem.at[0])
-    res_out.start()
+    tiles(lambda t: out_tile(t, mt[t], res))
+    leave(0).start()
     arrive(rec.at[6], 6)
     assemble(6, gmat)
     send_rows(lambda at: dot(inc.mr[at, :], gmat[...], 1, 1), 7)
@@ -357,41 +376,41 @@
     tiles(lambda t: pre_back_left(t, inc))
     arrive(rec.at[8], 8)
     unpack(8)
-    tiles(lambda t: pre_back_right(t, inc))
 
     def grad_middle_tile(t):
+        pre_back_right(t, inc)
         g = tail_back(t, ct[t], inc)
         gt[t] = g
         head_back(t, g, out)
 
     tiles(grad_middle_tile)
     send_staged(9)
-    proj_grads(inc, GRD)
+    proj_grads(inc, GRD, range(4))
     rows_of_grads(4, GRD, dot(inc.nb[...], inc.gg[...], 1, 1))
     rows_of_grads(5, GRD, dot(inc.ub[...], inc.gl[...], 1, 1))
     rows_of_grads(6, GRD, dot(out.nb[...], out.gg[...], 1, 1))
     rows_of_grads(7, GRD, dot(out.ub[...], out.gl[...], 1, 1))
     pack_grads(ga[0], GRD)
     arrive(rec.at[9], 9)
-    send_ready(ga[0], ga[1], 12)
     assemble(9, gmat)
     send_rows(lambda at: dot(gmat[at, :], out.mr[...], 1, 0), 10)
     send_rows(lambda at: dot(gmat[:, at], out.ml[...], 0, 0), 11)
-    arrive(ga[1], 12)
-    sum_grads(ga[1], ga[2], GRD)
+    send_ready(ga[0], ga[1], 12)
     arrive(rec.at[10], 10)
     unpack(10)
     tiles(lambda t: pre_back_left(t, out))
+    proj_grads(out, TAIL, (0, 1))
     arrive(rec.at[11], 11)
-    spread_grads(ga[2], 13)
     unpack(11)
     tiles(lambda t: pre_back_right(t, out))
-    proj_grads(out, TAIL)
+    proj_grads(out, TAIL, (2, 3))
     pack_grads(gb[0], TAIL)
     send_ready(gb[0], gb[1], 14)
-    tiles(lambda t: out_tile(t, tail_back(t, gt[t], out), grad_v))
-    grad_out = pltpu.make_async_copy(grad_v, grad, osem.at[1])
-    grad_out.start()
+    arrive(ga[1], 12)
+    sum_grads(ga[1], ga[2], GRD)
+    spread_grads(ga[2], 13)
+    tiles(lambda t: out_tile(t, tail_back(t, gt[t], out), grad))
+    leave(1).start()
     arrive(gb[1], 14)
     sum_grads(gb[1], gb[2], TAIL)
     spread_grads(gb[2], 15)
@@ -401,22 +420,25 @@
         write_rows(j, GRD, dpi.at[:, j * 128 : (j + 1) * 128])
     for j, dst in ((4, dgi), (5, dli), (6, dgo), (7, dlo)):
         write_rows(j, GRD, dst)
+    for j in range(3, 8):
+        leave(j).start()
     arrive(gb[2], 15)
     unpack_grads(gb[2], TAIL)
     for j in range(4):
         write_rows(j, TAIL, dpo.at[:, j * 128 : (j + 1) * 128])
+    leave(2).start()
 
     for k in range(12):
         drain(snd.at[k], ssem, k)
     for g, k in ((ga, 12), (gb, 14)):
         drain(g[0], ssem, k)
         drain(g[2], ssem, k + 1)
-    res_out.wait()
-    grad_out.wait()
-
-
-def scratch():
-    shapes = []
+    for j in range(8):
+        leave(j).wait()
+
+
+def scratch(arguments, results):
+    shapes = [pltpu.VMEM(v.shape, v.dtype) for v in arguments] + [pltpu.SemaphoreType.DMA((8,))]
     for _ in range(2):
         shapes += [pltpu.VMEM((TILES, 128, 128), F32)] * len(MODULE_FIELDS)
         shapes += [pltpu.VMEM((128, CELLS), BF16)] * len(FLAT_FIELDS)
@@ -436,8 +458,7 @@
         pltpu.VMEM((WIDE, WIDE), BF16),
         pltpu.VMEM((12, DEVICES, 3, 4, 128), BF16),
         pltpu.VMEM((12, DEVICES, 3, 4, 128), BF16),
-        pltpu.VMEM((BI, BK, C), F32),
-        pltpu.VMEM((BI, BK, C), F32),
+        pltpu.VMEM((TILES, 128, 128), F32),
         pltpu.VMEM((DEVICES * GRD, 128), F32),
     ]
     shapes += [pltpu.VMEM((DEVICES, GRD, 128), BF16)] * 3
@@ -445,9 +466,9 @@
     shapes += [
         pltpu.SemaphoreType.DMA((16,)),
         pltpu.SemaphoreType.DMA((16,)),
-        pltpu.SemaphoreType.DMA((2,)),
+        pltpu.SemaphoreType.DMA((8,)),
     ]
-    return shapes
+    return shapes + [pltpu.VMEM(v.shape, F32) for v in results]
 
 
 def publish(*refs):
@@ -464,7 +485,6 @@
 
 
 def local(*args):
-    vmem = pl.BlockSpec(memory_space=pltpu.VMEM)
     anywhere = pl.BlockSpec(memory_space=pl.ANY)
     pair = jax.ShapeDtypeStruct((BI, BK, C), F32)
     square = jax.ShapeDtypeStruct((C, C), F32)
@@ -473,9 +493,9 @@
     results = pl.pallas_call(
         kernel,
         out_shape=shapes,
-        in_specs=[vmem] * 8,
-        out_specs=(anywhere,) * 2 + (vmem,) * 6,
-        scratch_shapes=scratch(),
+        in_specs=[anywhere] * 8,
+        out_specs=(anywhere,) * 8,
+        scratch_shapes=scratch(args, shapes),
         compiler_params=pltpu.CompilerParams(
             has_side_effects=True, collective_id=0, vmem_limit_bytes=58 * 2**20
         ),

time: 126 us -> 124 us (0.984)
  Pallas kernels: 125 us -> 123 us
    pallas_call x1, Pallas kernels: 123 us -> 121 us  [local(): pl.pallas_call(kernel, out_shape=shapes, in_specs=[anywhere] * 8, out_spe...]
where the time goes in v4:
time: 124 us
  Pallas kernels  123 us (99%)
    pallas_call x1, Pallas kernels, local(): pl.pallas_call(kernel, out_shape=shapes, in_specs=[anywhere] * 8, out_spe...  121 us

profile of v4, /device:TPU:1, one launch (start us, length us, event | category | flops | bytes accessed | tf_op | source)
XLA Modules:
  0.0 124.0 jit_solution(2809757729226546216)
XLA Ops:
  0.6 120.8 %triangles.1 = (f32[24,48,128]{2,1,0:T(8,128)}, f32[24,48,128]{2,1,0:T(8,128)}, f32[128,512]{1,0:T(8,128)}, f32[128,128]{1,0:T(8,128)}, f32[128,128]{1,0:T(8,128...) custom-call(f32[24,48,128]{2,1,0:T(8,128)} %refs_0_.1, f32[24,48,128]{2,1,0:T(8,128)} %refs_1_.1, ...), custom_call_target="tpu_custom_call" | custom-call | tf_op jit(solution)/shard_map/triangles/pallas_call | solution.py:493
  121.4 2.5 %publish.1 = (f32[24,48,128]{2,1,0:T(8,128)}, f32[24,48,128]{2,1,0:T(8,128)}, f32[128,512]{1,0:T(8,128)}, f32[128,128]{1,0:T(8,128)}, f32[128,128]{1,0:T(8,128)}...) custom-call(f32[24,48,128]{2,1,0:T(8,128)} %get-tuple-element.16.refs_0_, ...), custom_call_target="tpu_custom_call" | custom-call | tf_op jit(solution)/shard_map/publish/pallas_call | solution.py:504

commit v5 on v4

--- a/solution.py
+++ b/solution.py
@@ -135,7 +135,7 @@
         lax.fori_loop(0, ROWS, step, 0)
 
     def tiles(body):
-        lax.fori_loop(0, TILES, lambda t, carry: (body(t), carry)[1], 0, unroll=4)
+        lax.fori_loop(0, TILES, lambda t, carry: (body(t), carry)[1], 0, unroll=6)
 
     low = lax.broadcasted_iota(jnp.int32, (BI, 128), 1) < SLOT
     top = lax.broadcasted_iota(jnp.int32, (BI, 128), 0) < TILES
@@ -378,12 +378,11 @@
     unpack(8)
 
     def grad_middle_tile(t):
-        pre_back_right(t, inc)
-        g = tail_back(t, ct[t], inc)
-        gt[t] = g
-        head_back(t, g, out)
-
+        gt[t] = tail_back(t, ct[t], inc)
+
+    tiles(lambda t: pre_back_right(t, inc))
     tiles(grad_middle_tile)
+    tiles(lambda t: head_back(t, gt[t], out))
     send_staged(9)
     proj_grads(inc, GRD, range(4))
     rows_of_grads(4, GRD, dot(inc.nb[...], inc.gg[...], 1, 1))

time: 124 us -> 122 us (0.984)
  Pallas kernels: 123 us -> 121 us
    pallas_call x1, Pallas kernels: 121 us -> 119 us  [local(): pl.pallas_call(kernel, out_shape=shapes, in_specs=[anywhere] * 8, out_spe...]
where the time goes in v5:
time: 122 us
  Pallas kernels  121 us (99%)
    pallas_call x1, Pallas kernels, local(): pl.pallas_call(kernel, out_shape=shapes, in_specs=[anywhere] * 8, out_spe...  119 us
    pallas_call x1, Pallas kernels, local(): pl.pallas_call(publish, out_shape=shapes, in_specs=[anywhere] * 8, out_sp...  2.46 us

profile of v5, /device:TPU:1, one launch (start us, length us, event | category | flops | bytes accessed | tf_op | source)
XLA Modules:
  0.0 122.1 jit_solution(13473387444446110197)
XLA Ops:
  0.6 118.8 %triangles.1 = (f32[24,48,128]{2,1,0:T(8,128)}, f32[24,48,128]{2,1,0:T(8,128)}, f32[128,512]{1,0:T(8,128)}, f32[128,128]{1,0:T(8,128)}, f32[128,128]{1,0:T(8,128...) custom-call(f32[24,48,128]{2,1,0:T(8,128)} %refs_0_.1, f32[24,48,128]{2,1,0:T(8,128)} %refs_1_.1, ...), custom_call_target="tpu_custom_call" | custom-call | tf_op jit(solution)/shard_map/triangles/pallas_call | solution.py:492
  119.5 2.5 %publish.1 = (f32[24,48,128]{2,1,0:T(8,128)}, f32[24,48,128]{2,1,0:T(8,128)}, f32[128,512]{1,0:T(8,128)}, f32[128,128]{1,0:T(8,128)}, f32[128,128]{1,0:T(8,128)}...) custom-call(f32[24,48,128]{2,1,0:T(8,128)} %get-tuple-element.16.refs_0_, ...), custom_call_target="tpu_custom_call" | custom-call | tf_op jit(solution)/shard_map/publish/pallas_call | solution.py:503

commit v6 on v5

--- a/solution.py
+++ b/solution.py
@@ -132,7 +132,7 @@
                     stage[pl.ds(pl.multiple_of(p * SGL, SGL) + 4 * j, 4), :] = rec[k, p, j].astype(F32)
             return carry
 
-        lax.fori_loop(0, ROWS, step, 0)
+        lax.fori_loop(0, ROWS, step, 0, unroll=2)
 
     def tiles(body):
         lax.fori_loop(0, TILES, lambda t, carry: (body(t), carry)[1], 0, unroll=6)
@@ -166,7 +166,7 @@
                 whole[at, m * 128 : (m + 1) * 128] = jnp.concatenate(ls + [gap16], axis=0).astype(BF16)
             return carry
 
-        lax.fori_loop(0, ROWS // 2, step, 0)
+        lax.fori_loop(0, ROWS // 2, step, 0, unroll=2)
 
     half = row // 4
 
@@ -289,7 +289,7 @@
                 snd[a * COLS + b] = ws[pl.ds(at, size), :].astype(BF16)
             return carry
 
-        lax.fori_loop(0, ROWS, step, 0)
+        lax.fori_loop(0, ROWS, step, 0, unroll=2)
 
     def sum_grads(rec, whole, size):
         whole[me] = lax.fori_loop(
@@ -309,7 +309,7 @@
                 ws[pl.ds(at, size), :] = whole[a * COLS + b].astype(F32)
             return carry
 
-        lax.fori_loop(0, ROWS, step, 0)
+        lax.fori_loop(0, ROWS, step, 0, unroll=2)
 
     def write_rows(j, size, dst):
         dst[...] = ws[pl.ds(j, 128, stride=size), :]

time: 122 us -> 121 us (level)
    pallas_call x1, Pallas kernels: 119 us -> 117 us  [local(): pl.pallas_call(kernel, out_shape=shapes, in_specs=[anywhere] * 8, out_spe...]
where the time goes in v6:
time: 121 us
  Pallas kernels  120 us (99%)
    pallas_call x1, Pallas kernels, local(): pl.pallas_call(kernel, out_shape=shapes, in_specs=[anywhere] * 8, out_spe...  117 us
    pallas_call x1, Pallas kernels, local(): pl.pallas_call(publish, out_shape=shapes, in_specs=[anywhere] * 8, out_sp...  2.46 us

profile of v6, /device:TPU:1, one launch (start us, length us, event | category | flops | bytes accessed | tf_op | source)
XLA Modules:
  0.0 120.6 jit_solution(3886132410754010770)
XLA Ops:
  0.6 117.3 %triangles.1 = (f32[24,48,128]{2,1,0:T(8,128)}, f32[24,48,128]{2,1,0:T(8,128)}, f32[128,512]{1,0:T(8,128)}, f32[128,128]{1,0:T(8,128)}, f32[128,128]{1,0:T(8,128...) custom-call(f32[24,48,128]{2,1,0:T(8,128)} %refs_0_.1, f32[24,48,128]{2,1,0:T(8,128)} %refs_1_.1, ...), custom_call_target="tpu_custom_call" | custom-call | tf_op jit(solution)/shard_map/triangles/pallas_call | solution.py:492
  117.9 2.5 %publish.1 = (f32[24,48,128]{2,1,0:T(8,128)}, f32[24,48,128]{2,1,0:T(8,128)}, f32[128,512]{1,0:T(8,128)}, f32[128,128]{1,0:T(8,128)}, f32[128,128]{1,0:T(8,128)}...) custom-call(f32[24,48,128]{2,1,0:T(8,128)} %get-tuple-element.16.refs_0_, ...), custom_call_target="tpu_custom_call" | custom-call | tf_op jit(solution)/shard_map/publish/pallas_call | solution.py:503
